TPU v7x, 512 devices: a whole 4x4x16 slice. The times are simulated.
512 devices in a mesh: ctx: 64 (over z_lo, x, core), head: 8 (over y, z_hi).
Axes of the slice: x: 4, y: 4, z: 16 (z_hi: 2, z_lo: 8; z = z_hi * 8 + z_lo), core: 2. Of those that a mesh axis runs over, the one named last changes fastest.
Arguments:
- queries: bfloat16 [32768, 4096], P('ctx', 'head'), may hold values from -6 to 6
- key_vectors: bfloat16 [32768, 4096], P('ctx', 'head'), may hold values from -6 to 6
- values: bfloat16 [32768, 4096], P('ctx', 'head'), may hold values from -30 to 30
- norm_gain: float32 [4096], P('head'), may hold values from 0.1 to 1.9
- cotangent: bfloat16 [32768, 4096], P('ctx', 'head'), may hold values from -8 to 8
Outputs:
- normed_out: bfloat16 [32768, 4096], P('ctx', 'head')
- query_grad: bfloat16 [32768, 4096], P('ctx', 'head')
- key_grad: bfloat16 [32768, 4096], P('ctx', 'head')
- value_grad: bfloat16 [32768, 4096], P('ctx', 'head')
All inputs are finite; a program needn't handle non-finite values.
Results may differ from a plain program's by a relative error of at most 0.015.
Values may be sent and summed in bfloat16 or wider, within the bound.
No kernel may reach another device: no remote copies, remote signals or barrier semaphores. Data moves between devices by JAX's collectives and lax.ppermute only.
A program may use at most 64 MiB of HBM per device.

v0:
```python
import jax
import jax.numpy as jnp
from jax import lax
from jax.sharding import PartitionSpec as P

DH = 128


EPSILON = 1e-05


def prefix(value, axis, join, neutral, backward):
    count = lax.axis_size(axis)
    place = lax.axis_index(axis)
    ahead = count - 1 - place if backward else place
    gathered = lax.all_gather(value.astype(jnp.bfloat16), axis)
    state = jnp.zeros_like(value) + jnp.asarray(neutral, value.dtype)

    def one(step, state):
        source = count - 1 - step if backward else step
        return join(state, lax.dynamic_index_in_dim(gathered, source, 0, False).astype(value.dtype))

    return lax.fori_loop(0, ahead, one, state)


def on_device(queries, key_vectors, values, norm_gain, cotangent):
    row_count = queries.shape[0]
    channels = queries.shape[1]
    local_heads = channels // DH
    full_width = channels * lax.axis_size("head")

    def split_heads(tensor):
        return tensor.reshape(row_count, local_heads, DH)

    query_heads = split_heads(queries)
    key_heads = split_heads(key_vectors)
    value_heads = split_heads(values)
    causal = lax.broadcasted_iota(jnp.int32, (row_count, row_count), 0) >= lax.broadcasted_iota(
        jnp.int32, (row_count, row_count), 1
    )
    own_state = jnp.einsum(
        "thd,the->hde", key_heads, value_heads, preferred_element_type=jnp.float32
    )
    prefix_state = prefix(own_state, "ctx", jnp.add, jnp.zeros_like(own_state), False)
    prefix_low = prefix_state.astype(jnp.bfloat16)
    scores = jnp.einsum("thd,shd->hts", query_heads, key_heads, preferred_element_type=jnp.float32)
    probs = jnp.where(causal[None], scores, 0.0).astype(jnp.bfloat16)
    intra = jnp.einsum("hts,shd->thd", probs, value_heads, preferred_element_type=jnp.float32)
    inter = jnp.einsum("thd,hde->the", query_heads, prefix_low, preferred_element_type=jnp.float32)
    attended = (intra + inter).reshape(row_count, channels)
    scaled = cotangent.astype(jnp.float32) * norm_gain
    squares = jnp.sum(attended * attended, axis=-1)
    slope_local = jnp.sum(scaled * attended, axis=-1)
    square_total = lax.psum(squares, "head")
    inverse = lax.rsqrt(square_total / full_width + EPSILON)[:, None]
    normed_out = (norm_gain * attended * inverse).astype(jnp.bfloat16)
    slope_total = lax.psum(slope_local, "head")
    slope = (slope_total / full_width)[:, None]
    attended_grad = (inverse * scaled - inverse * inverse * inverse * slope * attended).astype(
        jnp.bfloat16
    )
    grad_heads = split_heads(attended_grad)
    own_grad = jnp.einsum(
        "thd,the->hde", query_heads, grad_heads, preferred_element_type=jnp.float32
    )
    later_state = prefix(own_grad, "ctx", jnp.add, jnp.zeros_like(own_grad), True)
    later_low = later_state.astype(jnp.bfloat16)
    grad_scores = jnp.einsum(
        "the,she->hts", grad_heads, value_heads, preferred_element_type=jnp.float32
    )
    grad_probs = jnp.where(causal[None], grad_scores, 0.0).astype(jnp.bfloat16)
    query_total = jnp.einsum(
        "hts,shd->thd", grad_probs, key_heads, preferred_element_type=jnp.float32
    ) + jnp.einsum("the,hde->thd", grad_heads, prefix_low, preferred_element_type=jnp.float32)
    key_total = jnp.einsum(
        "hts,thd->shd", grad_probs, query_heads, preferred_element_type=jnp.float32
    ) + jnp.einsum("she,hde->shd", value_heads, later_low, preferred_element_type=jnp.float32)
    value_total = jnp.einsum(
        "hts,the->she", probs, grad_heads, preferred_element_type=jnp.float32
    ) + jnp.einsum("shd,hde->she", key_heads, later_low, preferred_element_type=jnp.float32)
    query_grad = query_total.reshape(row_count, channels).astype(jnp.bfloat16)
    key_grad = key_total.reshape(row_count, channels).astype(jnp.bfloat16)
    value_grad = value_total.reshape(row_count, channels).astype(jnp.bfloat16)
    return (normed_out, query_grad, key_grad, value_grad)


def solution(mesh):
    placed = (P("ctx", "head"), P("ctx", "head"), P("ctx", "head"), P("head"), P("ctx", "head"))
    return jax.shard_map(
        on_device,
        mesh=mesh,
        in_specs=placed,
        out_specs=(P("ctx", "head"), P("ctx", "head"), P("ctx", "head"), P("ctx", "head")),
        check_vma=False,
    )
```

profile of v0, /device:TPU:1, one launch (start us, length us, event | category | flops | bytes accessed | tf_op | source)
XLA Modules:
  0.0 443.2 jit_solution(16172428205034959782)
XLA Ops:
  7.2 1.3 copy.105
  8.6 2.2 convolution_convert_fusion.1
  11.8 1.4 copy-done.1
  13.9 130.5 %all-gather.5.cloned.1.call-done = bf16[256,128,128]{2,1,0:T(8,128)(2,1)} async-done(((bf16[4,128,128]{2,1,0:T(8,128)(2,1)}), bf16[256,128,128]{2,1,0:T(8,128)(2,1)}) %all-gather.5.cloned.1.call-update) | async-done | bytes 8388624 | tf_op jit(solution)/shard_map/all_gather | solution.py:16
  144.5 1.0 while.22
  144.5 1.0 convert_add_fusion.4
  146.7 38.2 %all-reduce = (f32[512]{0:T(512)S(1)}, f32[512]{0:T(512)S(1)}) all-reduce(f32[512]{0:T(512)S(1)} %get-tuple-element.119, f32[512]{0:T(512)S(1)} %multiply_reduce_fusion), channel_id=1, replica_groups=mesh['ctx'=64,'head'=8] {'head'}, use_global_device_ids=true, to_apply=%region_3.4 | all-reduce | flops 1024 | bytes 8192 | tf_op jit(solution)/shard_map/psum | solution.py:54
  184.9 1.1 subtract_convert_fusion
  189.1 1.1 fusion.3
  190.1 2.0 copy.56
  192.2 1.5 fusion.32
  194.7 174.9 %all-gather.7.cloned.1.call-done = bf16[256,128,128]{2,1,0:T(8,128)(2,1)} async-done(((bf16[4,128,128]{2,1,0:T(8,128)(2,1)}), bf16[256,128,128]{2,1,0:T(8,128)(2,1)}) %all-gather.7.cloned.1.call-update) | async-done | bytes 8388624 | tf_op jit(solution)/shard_map/all_gather | solution.py:16
  369.6 61.2 %while.23 = (s32[]{:T(128)}, f32[4,128,128]{2,1,0:T(8,128)S(1)}, s32[]{:T(128)}, bf16[64,4,128,128]{3,2,1,0:T(8,128)(2,1)}, s32[]{:T(128)}, /*index=5*/s32[]{:T(128)}, s32[]{:T(128)}, s32[]{:T(128)}) while((s32[]{:T(128)}, f32[4,128,128]{2,1,0:T(8,128)S(1)}, s32[]{:T(128)}, bf16[64,4,128,128]{3,2,1,0:T(8,128)(2,1)}, s32[]{:T(128)}, ...), condition=%wide.region_7.8_spmd, body=%wide.region_6.7_spmd.sunk | while | flops 131078 | bytes 655503 | solution.py:23
  369.6 1.0 convert_add_fusion.5
  370.6 1.0 convert_add_fusion.5
  371.6 1.0 convert_add_fusion.5
  372.6 1.0 convert_add_fusion.5
  373.5 1.0 convert_add_fusion.5
  374.5 1.0 convert_add_fusion.5
  375.5 1.0 convert_add_fusion.5
  376.5 1.0 convert_add_fusion.5
  377.5 1.0 convert_add_fusion.5
  378.5 1.0 convert_add_fusion.5
  379.5 1.0 convert_add_fusion.5
  380.4 1.0 convert_add_fusion.5
  381.4 1.0 convert_add_fusion.5
  382.4 1.0 convert_add_fusion.5
  383.4 1.0 convert_add_fusion.5
  384.4 1.0 convert_add_fusion.5
  385.4 1.0 convert_add_fusion.5
  386.4 1.0 convert_add_fusion.5
  387.4 1.0 convert_add_fusion.5
  388.3 1.0 convert_add_fusion.5
  389.3 1.0 convert_add_fusion.5
  390.3 1.0 convert_add_fusion.5
  391.3 1.0 convert_add_fusion.5
  392.3 1.0 convert_add_fusion.5
  396.2 1.0 convert_add_fusion.5
  400.2 1.0 convert_add_fusion.5
  405.1 1.0 convert_add_fusion.5
  410.0 1.0 convert_add_fusion.5
  415.0 1.0 convert_add_fusion.5
  418.9 1.0 convert_add_fusion.5
  423.8 1.0 convert_add_fusion.5
  428.8 1.0 convert_add_fusion.5
  430.8 2.2 fusion.5
  433.0 2.0 copy.58
  435.4 1.0 copy.57
  (81 shorter events, 36.2 us)
Async XLA Ops:
  7.2 3.8 copy-start
  7.2 3.8 copy-start.12
  7.2 137.3 %all-gather.5.cloned.1.call-start = ((), (), s32[]{:S(2)}) async-start(), calls=%async_computation | async-start | bytes 8519680 | tf_op jit(solution)/shard_map/all_gather | solution.py:16
  8.6 2.4 copy-start.6
  10.8 358.8 %all-gather.7.cloned.1.call-start = ((), (), s32[]{:S(2)}) async-start(), calls=%async_computation.1 | async-start | bytes 8519680 | tf_op jit(solution)/shard_map/all_gather | solution.py:16
  11.0 0.8 copy-start.13
  11.0 2.2 copy-start.9
  11.7 1.4 copy-start.1
  145.5 1.0 copy-start.8
  145.5 1.0 copy-start.15
  184.9 2.4 copy-start.10
  186.0 1.3 copy-start.14
  186.5 1.7 copy-start.7
  188.2 1.9 copy-start.3
  189.1 3.1 copy-start.2
  192.2 2.0 copy-start.4
  194.2 236.6 %copy-start.5 = (f32[4,128,512]{2,1,0:T(8,128)S(1)}, f32[4,128,512]{2,1,0:T(8,128)}, u32[]{:S(2)}) copy-start(f32[4,128,512]{2,1,0:T(8,128)} %fusion.32) | copy-start | bytes 3145732
  430.7 4.3 copy-start.11
Sparse Core Ops, SparseCore 0:
  10.9 133.5 all-gather.4
  187.5 182.0 all-gather.6
where the time goes:
time: 445 us; the launch traced here: 443 us
  waiting for transfers between devices  305 us (69%)
  other arithmetic  62.1 us (14%)
  blocking collectives  38.2 us (9%)
  between operations  14.3 us (3%)
  matrix products  11.6 us (3%)
  local copies, waits for them, and re-layouts  10 us (2%)
    all_gather x2, waiting for transfers between devices, prefix(): gathered = lax.all_gather(value.astype(jnp.bfloat16), axis)  305 us
    add x63, other arithmetic, one(): join(state, lax.dynamic_index_in_dim(gathered, source, 0, False).astype(v...  60.7 us
    psum x1, blocking collectives, on_device(): square_total = lax.psum(squares, 'head')  38.2 us
  transfers between devices with their start and end apart: 2, of which 2 were waited for; matrix products, arithmetic and copies ran while one was open for 2% of the time, Pallas kernels for 0%

commit v1 on v0

v1 whole, which is shorter than its diff:
```python
import jax
import jax.numpy as jnp
from jax import lax
from jax.sharding import Mesh, PartitionSpec as P

DH = 128
EPSILON = 1e-05
PLANE = ("x", "core")
LINE = "z_lo"
CTX = ("z_lo", "x", "core")
HEAD = ("y", "z_hi")


def scan_states(state, backward):
    plane = lax.axis_size("x") * lax.axis_size("core")
    line = lax.axis_size(LINE)
    place = lax.axis_index(LINE)
    chunks = state.astype(jnp.bfloat16).reshape(plane, -1, DH)
    mine = lax.all_to_all(chunks, PLANE, 0, 0).astype(jnp.float32)
    order = range(plane - 1, -1, -1) if backward else range(plane)
    running = jnp.zeros(mine.shape[1:], jnp.float32)
    local = [None] * plane
    for member in order:
        local[member] = running
        running = running + mine[member]
    spread = jnp.broadcast_to(running.astype(jnp.bfloat16)[None], (line,) + running.shape)
    totals = lax.all_to_all(spread, LINE, 0, 0).astype(jnp.float32)
    index = jnp.arange(line)
    keep = index > place if backward else index < place
    outer = jnp.sum(jnp.where(keep[:, None, None], totals, 0.0), axis=0)
    low = jnp.stack([one + outer for one in local]).astype(jnp.bfloat16)
    return lax.all_to_all(low, PLANE, 0, 0).reshape(state.shape)


def on_device(queries, key_vectors, values, norm_gain, cotangent):
    row_count = queries.shape[0]
    channels = queries.shape[1]
    local_heads = channels // DH
    full_width = channels * lax.axis_size("y") * lax.axis_size("z_hi")
    members = lax.axis_size("y") * lax.axis_size("z_hi")

    def split_heads(tensor):
        return tensor.reshape(row_count, local_heads, DH)

    query_heads = split_heads(queries)
    key_heads = split_heads(key_vectors)
    value_heads = split_heads(values)
    causal = lax.broadcasted_iota(jnp.int32, (row_count, row_count), 0) >= lax.broadcasted_iota(
        jnp.int32, (row_count, row_count), 1
    )
    own_state = jnp.einsum(
        "thd,the->hde", key_heads, value_heads, preferred_element_type=jnp.float32
    )
    prefix_low = scan_states(own_state, False)
    scores = jnp.einsum("thd,shd->hts", query_heads, key_heads, preferred_element_type=jnp.float32)
    probs = jnp.where(causal[None], scores, 0.0).astype(jnp.bfloat16)
    intra = jnp.einsum("hts,shd->thd", probs, value_heads, preferred_element_type=jnp.float32)
    inter = jnp.einsum("thd,hde->the", query_heads, prefix_low, preferred_element_type=jnp.float32)
    attended = (intra + inter).reshape(row_count, channels)
    scaled = cotangent.astype(jnp.float32) * norm_gain
    squares = jnp.sum(attended * attended, axis=-1)
    slope_local = jnp.sum(scaled * attended, axis=-1)
    both = jnp.concatenate([squares, slope_local]).reshape(1, -1, DH)
    both = lax.all_to_all(jnp.broadcast_to(both, (members,) + both.shape[1:]), HEAD, 0, 0)
    both = jnp.sum(both, axis=0).reshape(2, row_count) / full_width
    inverse = lax.rsqrt(both[0] + EPSILON)[:, None]
    normed_out = (norm_gain * attended * inverse).astype(jnp.bfloat16)
    slope = both[1][:, None]
    attended_grad = (inverse * scaled - inverse * inverse * inverse * slope * attended).astype(
        jnp.bfloat16
    )
    grad_heads = split_heads(attended_grad)
    own_grad = jnp.einsum(
        "thd,the->hde", query_heads, grad_heads, preferred_element_type=jnp.float32
    )
    later_low = scan_states(own_grad, True)
    grad_scores = jnp.einsum(
        "the,she->hts", grad_heads, value_heads, preferred_element_type=jnp.float32
    )
    grad_probs = jnp.where(causal[None], grad_scores, 0.0).astype(jnp.bfloat16)
    query_total = jnp.einsum(
        "hts,shd->thd", grad_probs, key_heads, preferred_element_type=jnp.float32
    ) + jnp.einsum("the,hde->thd", grad_heads, prefix_low, preferred_element_type=jnp.float32)
    key_total = jnp.einsum(
        "hts,thd->shd", grad_probs, query_heads, preferred_element_type=jnp.float32
    ) + jnp.einsum("she,hde->shd", value_heads, later_low, preferred_element_type=jnp.float32)
    value_total = jnp.einsum(
        "hts,the->she", probs, grad_heads, preferred_element_type=jnp.float32
    ) + jnp.einsum("shd,hde->she", key_heads, later_low, preferred_element_type=jnp.float32)
    query_grad = query_total.reshape(row_count, channels).astype(jnp.bfloat16)
    key_grad = key_total.reshape(row_count, channels).astype(jnp.bfloat16)
    value_grad = value_total.reshape(row_count, channels).astype(jnp.bfloat16)
    return (normed_out, query_grad, key_grad, value_grad)


def solution(mesh):
    fine = Mesh(
        mesh.devices.reshape(8, 4, 2, 4, 2), ("z_lo", "x", "core", "y", "z_hi")
    )
    placed = (P(CTX, HEAD), P(CTX, HEAD), P(CTX, HEAD), P(HEAD), P(CTX, HEAD))
    return jax.shard_map(
        on_device,
        mesh=fine,
        in_specs=placed,
        out_specs=(P(CTX, HEAD),) * 4,
        check_vma=False,
    )
```

time: 445 us -> 144 us (0.32)
  waiting for transfers between devices: 305 us -> 40.4 us
  starting transfers between devices: 0.08 us -> 49.9 us
  other arithmetic: 62.1 us -> 20.9 us
  blocking collectives: 38.2 us -> 0 us
  between operations: 14.3 us -> 0.83 us
  matrix products: 11.6 us -> 19.8 us
    all_gather x2 -> x0, waiting for transfers between devices: 305 us -> none  [prefix(): gathered = lax.all_gather(value.astype(jnp.bfloat16), axis)]
    add x63 -> x0, other arithmetic: 60.7 us -> none  [one(): join(state, lax.dynamic_index_in_dim(gathered, source, 0, False).astype(v...]
    all_to_all x0 -> x7, starting transfers between devices: none -> 49.9 us  [the longest x2 16.3 us: scan_states(): mine = lax.all_to_all(chunks, PLANE, 0, 0).astype(jnp.float32)]
    all_to_all x0 -> x7, waiting for transfers between devices: none -> 40.4 us  [the longest x1 13.8 us: on_device(): lax.all_to_all(jnp.broadcast_to(both, (members,) + both.shape[1:]), HEAD,...]
    psum x1 -> x0, blocking collectives: 38.2 us -> none  [on_device(): square_total = lax.psum(squares, 'head')]
    unnamed x0 -> x14, other arithmetic: none -> 14 us
  transfers between devices with their start and end apart: 2 -> 7, of which waited for: 2 -> 7; matrix products, arithmetic and copies ran while one was open for 2% -> 10% of each run, Pallas kernels for 0% -> 0%
where the time goes in v1:
time: 144 us; the launch traced here: 142 us
  starting transfers between devices  49.9 us (35%)
  waiting for transfers between devices  40.4 us (28%)
  other arithmetic  20.9 us (15%)
  matrix products  19.8 us (14%)
  local copies, waits for them, and re-layouts  10.2 us (7%)
    all_to_all x2, starting transfers between devices, scan_states(): mine = lax.all_to_all(chunks, PLANE, 0, 0).astype(jnp.float32)  16.3 us
    unnamed x14, other arithmetic  14 us
    all_to_all x1, waiting for transfers between devices, on_device(): lax.all_to_all(jnp.broadcast_to(both, (members,) + both.shape[1:]), HEAD,...  13.8 us
    all_to_all x2, waiting for transfers between devices, scan_states(): totals = lax.all_to_all(spread, LINE, 0, 0).astype(jnp.float32)  13.4 us
    all_to_all x2, starting transfers between devices, scan_states(): totals = lax.all_to_all(spread, LINE, 0, 0).astype(jnp.float32)  11.9 us
    all_to_all x2, starting transfers between devices, scan_states(): return lax.all_to_all(low, PLANE, 0, 0).reshape(state.shape)  11.7 us
    all_to_all x1, starting transfers between devices, on_device(): lax.all_to_all(jnp.broadcast_to(both, (members,) + both.shape[1:]), HEAD,...  9.94 us
    all_to_all x2, waiting for transfers between devices, scan_states(): mine = lax.all_to_all(chunks, PLANE, 0, 0).astype(jnp.float32)  8.89 us
  transfers between devices with their start and end apart: 7, of which 7 were waited for; matrix products, arithmetic and copies ran while one was open for 10% of the time, Pallas kernels for 0%

profile of v1, /device:TPU:1, one launch (start us, length us, event | category | flops | bytes accessed | tf_op | source)
XLA Modules:
  0.0 142.0 jit_solution(17831014381802347642)
XLA Ops:
  0.7 1.3 copy.111
  2.0 0.9 convolution_convert_fusion.1
  3.0 10.2 %all-to-all-start = ((bf16[8,64,128]{2,1,0:T(8,128)(2,1)}), bf16[8,64,128]{2,1,0:T(8,128)(2,1)S(1)}, u32[]{:S(2)}, u32[]{:S(2)}) async-start(bf16[8,64,128]{2,1,0:T(8,128)(2,1)} %bitcast.1), calls=%async_computation | async-start | bytes 262144 | tf_op jit(solution)/shard_map/all_to_all | solution.py:19
  13.1 5.3 %all-to-all-done = bf16[8,64,128]{2,1,0:T(8,128)(2,1)S(1)} async-done(((bf16[8,64,128]{2,1,0:T(8,128)(2,1)}), bf16[8,64,128]{2,1,0:T(8,128)(2,1)S(1)}, u32[]{:S(2)}, u32[]{:S(2)}) %all-to-all-start) | async-done | bytes 131104 | tf_op jit(solution)/shard_map/all_to_all | solution.py:19
  18.4 0.6 fusion.34
  19.1 0.7 broadcast_in_dim.68
  19.7 7.9 %all-to-all-start.1 = ((bf16[8,64,128]{2,1,0:T(8,128)(2,1)}), bf16[8,64,128]{2,1,0:T(8,128)(2,1)S(1)}, u32[]{:S(2)}, u32[]{:S(2)}) async-start(bf16[8,64,128]{2,1,0:T(8,128)(2,1)} %broadcast_in_dim.68), calls=%async_computation.1 | async-start | bytes 262144 | tf_op jit(solution)/shard_map/all_to_all | solution.py:27
  28.0 0.8 copy-done.10
  28.7 1.9 %select_convert_fusion.1 = bf16[4,512,512]{2,1,0:T(8,128)(2,1)S(1)} fusion(bf16[512,4,128]{0,2,1:T(8,128)(2,1)S(1)} %bitcast.183, pred[512,512]{1,0:T(8,128)(4,1)S(1)} %iota_compare_fusion, bf16[512,512]{1,0:T(8,128)(2,1)} %param.6), kind=kOutput, calls=%fused_computation.1 | convolution fusion | flops 270532608 | bytes 3407872 | tf_op jit(solution)/shard_map/thd,shd->hts/dot_general | solution.py:55
  30.6 7.3 %all-to-all-done.1 = bf16[8,64,128]{2,1,0:T(8,128)(2,1)S(1)} async-done(((bf16[8,64,128]{2,1,0:T(8,128)(2,1)}), bf16[8,64,128]{2,1,0:T(8,128)(2,1)S(1)}, u32[]{:S(2)}, u32[]{:S(2)}) %all-to-all-start.1) | async-done | bytes 131104 | tf_op jit(solution)/shard_map/all_to_all | solution.py:27
  39.9 0.6 constant_dynamic-update-slice_fusion.4
  40.5 1.4 constant_dynamic-update-slice_fusion.3
  41.9 1.4 constant_dynamic-update-slice_fusion.2
  43.2 1.4 constant_dynamic-update-slice_fusion.1
  44.6 1.4 constant_dynamic-update-slice_fusion
  46.0 5.9 %all-to-all-start.2 = ((bf16[8,64,128]{2,1,0:T(8,128)(2,1)}), bf16[8,64,128]{2,1,0:T(8,128)(2,1)S(1)}, u32[]{:S(2)}, u32[]{:S(2)}) async-start(bf16[8,64,128]{2,1,0:T(8,128)(2,1)} %constant_dynamic-update-slice_fusion), calls=%async_computation.2 | async-start | bytes 262144 | tf_op jit(solution)/shard_map/all_to_all | solution.py:32
  51.8 1.8 %convolution_bitcast_fusion.2 = f32[512,4,128]{0,2,1:T(8,128)} fusion(bf16[4,512,512]{2,1,0:T(8,128)(2,1)S(1)} %select_convert_fusion.1, bf16[512,512]{1,0:T(8,128)(2,1)S(1)} %copy-done), kind=kOutput, calls=%fused_computation.4 | convolution fusion | flops 268435456 | bytes 3670016 | tf_op jit(solution)/shard_map/hts,shd->thd/dot_general | solution.py:57
  53.6 3.5 %all-to-all-done.2 = bf16[8,64,128]{2,1,0:T(8,128)(2,1)S(1)} async-done(((bf16[8,64,128]{2,1,0:T(8,128)(2,1)}), bf16[8,64,128]{2,1,0:T(8,128)(2,1)S(1)}, u32[]{:S(2)}, u32[]{:S(2)}) %all-to-all-start.2) | async-done | bytes 131104 | tf_op jit(solution)/shard_map/all_to_all | solution.py:32
  57.1 1.6 %multiply_reduce_fusion.1 = (f32[512]{0:T(512)S(1)}, f32[512,4,128]{0,2,1:T(8,128)S(1)}) fusion(f32[512,4,128]{0,2,1:T(8,128)} %convolution_bitcast_fusion.2, bf16[4,128,128]{2,1,0:T(8,128)(2,1)S(1)} %bitcast.193, bf16[512,4,128]{0,2,1:T(8,128)(2,1)S(1)} %bitcast.184), kind=kOutput, calls=%fused_computation.21 | convolution fusion | flops 67894784 | bytes 2754560 | tf_op jit(solution)/shard_map/thd,hde->the/dot_general | solution.py:58
  59.4 0.6 broadcast_in_dim.70
  60.0 9.9 %all-to-all-start.3 = ((f32[8,8,128]{2,1,0:T(8,128)}), f32[8,8,128]{2,1,0:T(8,128)S(1)}, u32[]{:S(2)}, u32[]{:S(2)}) async-start(f32[8,8,128]{2,1,0:T(8,128)} %broadcast_in_dim.70), calls=%async_computation.3 | async-start | bytes 65536 | tf_op jit(solution)/shard_map/all_to_all | solution.py:64
  69.9 13.8 %all-to-all-done.3 = f32[8,8,128]{2,1,0:T(8,128)S(1)} async-done(((f32[8,8,128]{2,1,0:T(8,128)}), f32[8,8,128]{2,1,0:T(8,128)S(1)}, u32[]{:S(2)}, u32[]{:S(2)}) %all-to-all-start.3) | async-done | bytes 32800 | tf_op jit(solution)/shard_map/all_to_all | solution.py:64
  83.8 1.3 subtract_convert_fusion
  85.1 1.4 copy.84
  86.5 2.0 %convolution_convert_fusion = bf16[4,128,128]{1,2,0:T(8,128)(2,1)} fusion(bf16[512,4,128]{0,2,1:T(8,128)(2,1)} %bitcast.185, bf16[512,4,128]{0,2,1:T(8,128)(2,1)S(1)} %bitcast.179), kind=kOutput, calls=%fused_computation.15 | convolution fusion | flops 67174400 | bytes 1179648 | tf_op jit(solution)/shard_map/thd,the->hde/dot_general | solution.py:73
  88.5 1.4 %fusion.37 = f32[4,128,512]{2,1,0:T(8,128)} fusion(bf16[512,4,128]{0,2,1:T(8,128)(2,1)S(1)} %bitcast.180, bf16[4,512,512]{2,1,0:T(8,128)(2,1)S(1)} %copy-done.2), kind=kOutput, calls=%fused_computation.108 | convolution fusion | flops 268435456 | bytes 3670016 | tf_op jit(solution)/shard_map/hts,the->she/dot_general | solution.py:87
  89.9 6.2 %all-to-all-start.4 = ((bf16[8,64,128]{2,1,0:T(8,128)(2,1)}), bf16[8,64,128]{2,1,0:T(8,128)(2,1)}, u32[]{:S(2)}, u32[]{:S(2)}) async-start(bf16[8,64,128]{2,1,0:T(8,128)(2,1)} %bitcast.16), calls=%async_computation.4 | async-start | bytes 262144 | tf_op jit(solution)/shard_map/all_to_all | solution.py:19
  96.1 1.8 %select_convert_fusion = bf16[4,512,512]{2,1,0:T(8,128)(2,1)S(1)} fusion(bf16[512,4,128]{0,2,1:T(8,128)(2,1)S(1)} %bitcast.181, pred[512,512]{1,0:T(8,128)(4,1)} %copy-done.10, bf16[512,512]{1,0:T(8,128)(2,1)S(1)} %copy-done), kind=kOutput, calls=%fused_computation | convolution fusion | flops 270532608 | bytes 3407872 | tf_op jit(solution)/shard_map/the,she->hts/dot_general | solution.py:77
  97.9 3.6 %all-to-all-done.4 = bf16[8,64,128]{2,1,0:T(8,128)(2,1)} async-done(((bf16[8,64,128]{2,1,0:T(8,128)(2,1)}), bf16[8,64,128]{2,1,0:T(8,128)(2,1)}, u32[]{:S(2)}, u32[]{:S(2)}) %all-to-all-start.4) | async-done | bytes 131104 | tf_op jit(solution)/shard_map/all_to_all | solution.py:19
  101.5 0.9 convert_element_type.80
  102.4 0.6 fusion.35
  103.0 0.7 broadcast_in_dim.73
  103.7 4.0 %all-to-all-start.5 = ((bf16[8,64,128]{2,1,0:T(8,128)(2,1)}), bf16[8,64,128]{2,1,0:T(8,128)(2,1)}, u32[]{:S(2)}, u32[]{:S(2)}) async-start(bf16[8,64,128]{2,1,0:T(8,128)(2,1)} %broadcast_in_dim.73), calls=%async_computation.5 | async-start | bytes 262144 | tf_op jit(solution)/shard_map/all_to_all | solution.py:27
  107.7 2.5 %convolution_bitcast_fusion = f32[512,4,128]{0,2,1:T(8,128)} fusion(bf16[512,4,128]{0,2,1:T(8,128)(2,1)} %bitcast.186, bf16[4,512,512]{2,1,0:T(8,128)(2,1)S(1)} %select_convert_fusion), kind=kOutput, calls=%fused_computation.2 | convolution fusion | flops 268435456 | bytes 3670016 | tf_op jit(solution)/shard_map/hts,thd->shd/dot_general | solution.py:84
  110.3 1.8 %convolution_bitcast_fusion.1 = f32[512,4,128]{0,2,1:T(8,128)} fusion(bf16[4,512,512]{2,1,0:T(8,128)(2,1)S(1)} %select_convert_fusion, bf16[512,4,128]{0,2,1:T(8,128)(2,1)S(1)} %bitcast.189), kind=kOutput, calls=%fused_computation.3 | convolution fusion | flops 268435456 | bytes 3670016 | tf_op jit(solution)/shard_map/hts,shd->thd/dot_general | solution.py:81
  112.0 6.1 %all-to-all-done.5 = bf16[8,64,128]{2,1,0:T(8,128)(2,1)} async-done(((bf16[8,64,128]{2,1,0:T(8,128)(2,1)}), bf16[8,64,128]{2,1,0:T(8,128)(2,1)}, u32[]{:S(2)}, u32[]{:S(2)}) %all-to-all-start.5) | async-done | bytes 131104 | tf_op jit(solution)/shard_map/all_to_all | solution.py:27
  118.1 1.0 select_reduce_fusion
  119.1 1.4 constant_dynamic-update-slice_fusion.15
  120.5 1.5 %constant_dynamic-update-slice_fusion.14 = bf16[8,64,128]{2,1,0:T(8,128)(2,1)} fusion(bf16[8,64,128]{2,1,0:T(8,128)(2,1)} %constant_dynamic-update-slice_fusion.15, f32[1,64,128]{2,1,0:T(8,128)} %get-tuple-element.17, f32[64,128]{1,0:T(8,128)S(1)} %select_reduce_fusion), kind=kLoop, calls=%fused_computation.51 | loop fusion | flops 16384 | bytes 81920
  122.0 1.4 constant_dynamic-update-slice_fusion.13
  123.3 1.4 constant_dynamic-update-slice_fusion.12
  127.2 5.9 %all-to-all-start.6 = ((bf16[8,64,128]{2,1,0:T(8,128)(2,1)}), bf16[8,64,128]{2,1,0:T(8,128)(2,1)S(1)}, u32[]{:S(2)}, u32[]{:S(2)}) async-start(bf16[8,64,128]{2,1,0:T(8,128)(2,1)} %constant_dynamic-update-slice_fusion.8), calls=%async_computation.6 | async-start | bytes 262144 | tf_op jit(solution)/shard_map/all_to_all | solution.py:32
  133.0 2.3 %fusion.3 = bf16[512,4,128]{0,2,1:T(8,128)(2,1)} fusion(f32[512,4,128]{0,2,1:T(8,128)} %convolution_bitcast_fusion.1, bf16[4,128,128]{2,1,0:T(8,128)(2,1)S(1)} %bitcast.194, bf16[512,4,128]{0,2,1:T(8,128)(2,1)S(1)} %bitcast.182), kind=kOutput, calls=%fused_computation.12 | convolution fusion | flops 67633152 | bytes 2228224 | tf_op jit(solution)/shard_map/the,hde->thd/dot_general | solution.py:83
  135.3 2.1 %copy.78 = bf16[512,512]{1,0:T(8,128)(2,1)} copy(bf16[512,512]{0,1:T(8,128)(2,1)} %bitcast.190) | data formatting | bytes 1048576
  137.5 0.9 all-to-all-done.6
  138.3 1.4 fusion.5
  139.7 1.0 copy.80
  141.0 1.0 copy.79
  (44 shorter events, 5.6 us)
Async XLA Ops:
  0.6 1.4 copy-start
  0.6 27.0 %copy-start.9 = (bf16[512,512]{1,0:T(8,128)(2,1)S(1)}, bf16[512,512]{1,0:T(8,128)(2,1)}, u32[]{:S(2)}) copy-start(bf16[512,512]{1,0:T(8,128)(2,1)} %param.5) | copy-start | bytes 1572868
  2.0 11.1 %copy-start.6 = (bf16[512,512]{0,1:T(8,128)(2,1)}, bf16[512,512]{0,1:T(8,128)(2,1)S(1)}, u32[]{:S(2)}) copy-start(bf16[512,512]{0,1:T(8,128)(2,1)S(1)} %copy.111) | copy-start | bytes 1572868
  3.0 15.4 %all-to-all-start = ((bf16[8,64,128]{2,1,0:T(8,128)(2,1)}), bf16[8,64,128]{2,1,0:T(8,128)(2,1)S(1)}, u32[]{:S(2)}, u32[]{:S(2)}) async-start(bf16[8,64,128]{2,1,0:T(8,128)(2,1)} %bitcast.1), calls=%async_computation | async-start | bytes 262144 | tf_op jit(solution)/shard_map/all_to_all | solution.py:19
  19.7 18.2 %all-to-all-start.1 = ((bf16[8,64,128]{2,1,0:T(8,128)(2,1)}), bf16[8,64,128]{2,1,0:T(8,128)(2,1)S(1)}, u32[]{:S(2)}, u32[]{:S(2)}) async-start(bf16[8,64,128]{2,1,0:T(8,128)(2,1)} %broadcast_in_dim.68), calls=%async_computation.1 | async-start | bytes 262144 | tf_op jit(solution)/shard_map/all_to_all | solution.py:27
  27.9 29.3 %copy-start.3 = (bf16[512,512]{0,1:T(8,128)(2,1)}, bf16[512,512]{0,1:T(8,128)(2,1)S(1)}, u32[]{:S(2)}) copy-start(bf16[512,512]{0,1:T(8,128)(2,1)S(1)} %copy.83) | copy-start | bytes 1572868
  28.0 0.8 copy-start.10
  30.6 23.0 %copy-start.1 = (bf16[4,512,512]{2,1,0:T(8,128)(2,1)}, bf16[4,512,512]{2,1,0:T(8,128)(2,1)S(1)}, u32[]{:S(2)}) copy-start(bf16[4,512,512]{2,1,0:T(8,128)(2,1)S(1)} %select_convert_fusion.1) | copy-start | bytes 6291460
  46.0 11.2 %all-to-all-start.2 = ((bf16[8,64,128]{2,1,0:T(8,128)(2,1)}), bf16[8,64,128]{2,1,0:T(8,128)(2,1)S(1)}, u32[]{:S(2)}, u32[]{:S(2)}) async-start(bf16[8,64,128]{2,1,0:T(8,128)(2,1)} %constant_dynamic-update-slice_fusion), calls=%async_computation.2 | async-start | bytes 262144 | tf_op jit(solution)/shard_map/all_to_all | solution.py:32
  57.1 2.0 %copy-start.8 = (bf16[512,512]{1,0:T(8,128)(2,1)S(1)}, bf16[512,512]{1,0:T(8,128)(2,1)}, u32[]{:S(2)}) copy-start(bf16[512,512]{1,0:T(8,128)(2,1)} %param.9) | copy-start | bytes 1572868
  57.1 2.0 %copy-start.11 = (f32[512]{0:T(512)S(1)}, f32[512]{0:T(512)}, u32[]{:S(2)}) copy-start(f32[512]{0:T(512)} %param.8) | copy-start | bytes 6148
  60.0 23.8 %all-to-all-start.3 = ((f32[8,8,128]{2,1,0:T(8,128)}), f32[8,8,128]{2,1,0:T(8,128)S(1)}, u32[]{:S(2)}, u32[]{:S(2)}) async-start(f32[8,8,128]{2,1,0:T(8,128)} %broadcast_in_dim.70), calls=%async_computation.3 | async-start | bytes 65536 | tf_op jit(solution)/shard_map/all_to_all | solution.py:64
  85.1 3.4 %copy-start.2 = (bf16[4,512,512]{2,1,0:T(8,128)(2,1)S(1)}, bf16[4,512,512]{2,1,0:T(8,128)(2,1)}, u32[]{:S(2)}) copy-start(bf16[4,512,512]{2,1,0:T(8,128)(2,1)} %copy-done.1) | copy-start | bytes 6291460
  89.9 11.6 %all-to-all-start.4 = ((bf16[8,64,128]{2,1,0:T(8,128)(2,1)}), bf16[8,64,128]{2,1,0:T(8,128)(2,1)}, u32[]{:S(2)}, u32[]{:S(2)}) async-start(bf16[8,64,128]{2,1,0:T(8,128)(2,1)} %bitcast.16), calls=%async_computation.4 | async-start | bytes 262144 | tf_op jit(solution)/shard_map/all_to_all | solution.py:19
  103.7 14.4 %all-to-all-start.5 = ((bf16[8,64,128]{2,1,0:T(8,128)(2,1)}), bf16[8,64,128]{2,1,0:T(8,128)(2,1)}, u32[]{:S(2)}, u32[]{:S(2)}) async-start(bf16[8,64,128]{2,1,0:T(8,128)(2,1)} %broadcast_in_dim.73), calls=%async_computation.5 | async-start | bytes 262144 | tf_op jit(solution)/shard_map/all_to_all | solution.py:27
  107.7 2.5 %copy-start.7 = (bf16[512,512]{0,1:T(8,128)(2,1)S(1)}, bf16[512,512]{0,1:T(8,128)(2,1)}, u32[]{:S(2)}) copy-start(bf16[512,512]{0,1:T(8,128)(2,1)} %copy-done.6) | copy-start | bytes 1572868
  120.5 17.8 %copy-start.4 = (f32[4,128,512]{2,1,0:T(8,128)S(1)}, f32[4,128,512]{2,1,0:T(8,128)}, u32[]{:S(2)}) copy-start(f32[4,128,512]{2,1,0:T(8,128)} %fusion.37) | copy-start | bytes 3145732
  127.2 11.2 %all-to-all-start.6 = ((bf16[8,64,128]{2,1,0:T(8,128)(2,1)}), bf16[8,64,128]{2,1,0:T(8,128)(2,1)S(1)}, u32[]{:S(2)}, u32[]{:S(2)}) async-start(bf16[8,64,128]{2,1,0:T(8,128)(2,1)} %constant_dynamic-update-slice_fusion.8), calls=%async_computation.6 | async-start | bytes 262144 | tf_op jit(solution)/shard_map/all_to_all | solution.py:32
  135.3 5.4 %copy-start.5 = (f32[512,4,128]{0,2,1:T(8,128)S(1)}, f32[512,4,128]{0,2,1:T(8,128)}, u32[]{:S(2)}) copy-start(f32[512,4,128]{0,2,1:T(8,128)} %convolution_bitcast_fusion) | copy-start | bytes 3145732

commit v2 on v1

v2 whole, which is shorter than its diff:
```python
import functools

import jax
import jax.numpy as jnp
from jax import lax
from jax.experimental import pallas as pl
from jax.experimental.pallas import tpu as pltpu
from jax.sharding import Mesh, PartitionSpec as P

DH = 128
EPSILON = 1e-05
PLANE = ("x", "core")
LINE = "z_lo"
CTX = ("z_lo", "x", "core")
HEAD = ("y", "z_hi")
LOW = jnp.bfloat16
WIDE = jnp.float32


def dot(left, right, left_dim, right_dim):
    return lax.dot_general(
        left, right, (((left_dim,), (right_dim,)), ((), ())), preferred_element_type=WIDE
    )


def head_columns(head):
    return slice(head * DH, (head + 1) * DH)


def state_of(low_ref, head):
    rows = low_ref.shape[1]
    per_head = DH // rows
    return low_ref[head * per_head : (head + 1) * per_head].reshape(DH, DH)


def put_state(out_ref, head, state):
    rows = out_ref.shape[1]
    per_head = DH // rows
    out_ref[head * per_head : (head + 1) * per_head] = state.astype(LOW).reshape(
        per_head, rows, DH
    )


def causal_tile(size):
    return lax.broadcasted_iota(jnp.int32, (size, size), 0) >= lax.broadcasted_iota(
        jnp.int32, (size, size), 1
    )


def own_state_kernel(left_ref, right_ref, out_ref):
    for head in range(left_ref.shape[1] // DH):
        at = head_columns(head)
        put_state(out_ref, head, dot(left_ref[:, at], right_ref[:, at], 0, 0))


def masked_tiles(left_ref, right_ref, at, out_ref, head):
    half = left_ref.shape[0] // 2
    causal = causal_tile(half)
    first = dot(left_ref[:, at], right_ref[:half, at], 1, 1)
    last = dot(left_ref[half:, at], right_ref[half:, at], 1, 1)
    out_ref[head, :half] = jnp.where(causal, first[:half], 0.0).astype(LOW)
    out_ref[head, half : 2 * half] = first[half:].astype(LOW)
    out_ref[head, 2 * half :] = jnp.where(causal, last, 0.0).astype(LOW)


def rows_product(tiles_ref, head, right_ref, at):
    half = tiles_ref.shape[2]
    both = dot(tiles_ref[head, : 2 * half], right_ref[:half, at], 1, 0)
    last = dot(tiles_ref[head, 2 * half :], right_ref[half:, at], 1, 0)
    return both[:half], both[half:] + last


def columns_product(tiles_ref, head, right_ref, at):
    half = tiles_ref.shape[2]
    first = dot(tiles_ref[head, : 2 * half], right_ref[:, at], 0, 0)
    last = dot(tiles_ref[head, 2 * half :], right_ref[half:, at], 0, 0)
    return first, last


def intra_kernel(query_ref, key_ref, value_ref, tiles_ref, intra_ref):
    half = query_ref.shape[0] // 2
    for head in range(query_ref.shape[1] // DH):
        at = head_columns(head)
        masked_tiles(query_ref, key_ref, at, tiles_ref, head)
        top, bottom = rows_product(tiles_ref, head, value_ref, at)
        intra_ref[:half, at] = top
        intra_ref[half:, at] = bottom


def totals_kernel(mine_ref, out_ref):
    total = mine_ref[0].astype(WIDE)
    for member in range(1, mine_ref.shape[0]):
        total = total + mine_ref[member].astype(WIDE)
    out_ref[...] = jnp.broadcast_to(total.astype(LOW)[None], out_ref.shape)


def chunks_kernel(backward, place_ref, mine_ref, totals_ref, out_ref):
    place = place_ref[0]
    running = jnp.zeros(mine_ref.shape[1:], WIDE)
    for plane in range(totals_ref.shape[0]):
        keep = plane > place if backward else plane < place
        running = running + jnp.where(keep, totals_ref[plane].astype(WIDE), 0.0)
    members = mine_ref.shape[0]
    for member in range(members - 1, -1, -1) if backward else range(members):
        out_ref[member] = running.astype(LOW)
        running = running + mine_ref[member].astype(WIDE)


def attend_kernel(query_ref, low_ref, intra_ref, cotangent_ref, gain_ref, attended_ref, sums_ref):
    rows, channels = query_ref.shape
    squares = jnp.zeros((rows, DH), WIDE)
    slopes = jnp.zeros((rows, DH), WIDE)
    for head in range(channels // DH):
        at = head_columns(head)
        attended = intra_ref[:, at] + dot(query_ref[:, at], state_of(low_ref, head), 1, 0)
        attended_ref[:, at] = attended
        squares = squares + attended * attended
        slopes = slopes + cotangent_ref[:, at].astype(WIDE) * gain_ref[:, at] * attended
    parts = []
    for sums in (squares, slopes):
        for block in range(rows // DH):
            turned = jnp.transpose(sums[block * DH : (block + 1) * DH])
            parts.append(jnp.sum(turned, axis=0, keepdims=True))
    packed = jnp.concatenate(parts, axis=0)
    sums_ref[...] = jnp.broadcast_to(packed[None], sums_ref.shape)


def grad_kernel(
    full_width, sums_ref, attended_ref, cotangent_ref, gain_ref, query_ref,
    grad_ref, own_ref, inverse_ref,
):
    rows, channels = query_ref.shape
    blocks = rows // DH
    total = sums_ref[0]
    for member in range(1, sums_ref.shape[0]):
        total = total + sums_ref[member]
    mean = total * (1.0 / full_width)
    inverse = lax.rsqrt(mean[:blocks] + EPSILON)
    factor = inverse * inverse * inverse * mean[blocks:]
    for block in range(blocks):
        at_rows = slice(block * DH, (block + 1) * DH)
        wide = jnp.transpose(jnp.broadcast_to(inverse[block : block + 1], (DH, DH)))
        second = jnp.transpose(jnp.broadcast_to(factor[block : block + 1], (DH, DH)))
        inverse_ref[at_rows] = wide
        for head in range(channels // DH):
            at = head_columns(head)
            scaled = cotangent_ref[at_rows, at].astype(WIDE) * gain_ref[:, at]
            grad_ref[at_rows, at] = (
                wide * scaled - second * attended_ref[at_rows, at]
            ).astype(LOW)
    for head in range(channels // DH):
        at = head_columns(head)
        put_state(own_ref, head, dot(query_ref[:, at], grad_ref[:, at], 0, 0))


def query_grad_kernel(
    grad_ref, key_ref, value_ref, low_ref, attended_ref, inverse_ref, gain_ref,
    grad_tiles_ref, query_grad_ref, normed_ref,
):
    half = grad_ref.shape[0] // 2
    inverse = inverse_ref[...]
    for head in range(grad_ref.shape[1] // DH):
        at = head_columns(head)
        masked_tiles(grad_ref, value_ref, at, grad_tiles_ref, head)
        inter = dot(grad_ref[:, at], state_of(low_ref, head), 1, 1)
        top, bottom = rows_product(grad_tiles_ref, head, key_ref, at)
        query_grad_ref[:half, at] = (top + inter[:half]).astype(LOW)
        query_grad_ref[half:, at] = (bottom + inter[half:]).astype(LOW)
        normed_ref[:, at] = (gain_ref[:, at] * attended_ref[:, at] * inverse).astype(LOW)


def partial_kernel(
    grad_ref, query_ref, tiles_ref, grad_tiles_ref, key_part_ref, value_part_ref
):
    half = grad_ref.shape[0] // 2
    for head in range(grad_ref.shape[1] // DH):
        at = head_columns(head)
        first, last = columns_product(grad_tiles_ref, head, query_ref, at)
        key_part_ref[:half, at] = first
        key_part_ref[half:, at] = last
        first, last = columns_product(tiles_ref, head, grad_ref, at)
        value_part_ref[:half, at] = first
        value_part_ref[half:, at] = last


def final_kernel(
    key_ref, value_ref, later_ref, key_part_ref, value_part_ref, key_grad_ref, value_grad_ref
):
    for head in range(key_ref.shape[1] // DH):
        at = head_columns(head)
        later = state_of(later_ref, head)
        key_grad_ref[:, at] = (
            key_part_ref[:, at] + dot(value_ref[:, at], later, 1, 1)
        ).astype(LOW)
        value_grad_ref[:, at] = (
            value_part_ref[:, at] + dot(key_ref[:, at], later, 1, 0)
        ).astype(LOW)


IN_VMEM = pl.BlockSpec(memory_space=pltpu.VMEM)
IN_SMEM = pl.BlockSpec(memory_space=pltpu.SMEM)


def call(kernel, shapes, *operands, flops=0, scalars=0, mib=8):
    outs = tuple(jax.ShapeDtypeStruct(shape, kind) for shape, kind in shapes)
    moved = sum(a.size * a.dtype.itemsize for a in operands) + sum(
        o.size * o.dtype.itemsize for o in outs
    )
    return pl.pallas_call(
        kernel,
        out_shape=outs,
        in_specs=[IN_SMEM] * scalars + [IN_VMEM] * (len(operands) - scalars),
        out_specs=tuple(IN_VMEM for _ in outs),
        compiler_params=pltpu.CompilerParams(vmem_limit_bytes=mib * 2**20),
        cost_estimate=pl.CostEstimate(flops=flops, bytes_accessed=moved, transcendentals=0),
    )(*operands)


def scan_states(chunks, place, backward):
    shape = (chunks.shape, LOW)
    line = lax.axis_size(LINE)
    mine = lax.all_to_all(chunks, PLANE, 0, 0)
    (spread,) = call(totals_kernel, [((line,) + mine.shape[1:], LOW)], mine)
    totals = lax.all_to_all(spread, LINE, 0, 0)
    (low,) = call(
        functools.partial(chunks_kernel, backward), [shape], place, mine, totals, scalars=1
    )
    return lax.all_to_all(low, PLANE, 0, 0)


def on_device(queries, key_vectors, values, norm_gain, cotangent):
    rows, channels = queries.shape
    heads = channels // DH
    half = rows // 2
    members = lax.axis_size("y") * lax.axis_size("z_hi")
    plane = lax.axis_size("x") * lax.axis_size("core")
    full_width = channels * members
    place = lax.axis_index(LINE).astype(jnp.int32).reshape(1)
    gain = norm_gain.reshape(1, channels)
    unit = 2 * rows * DH * DH * heads
    chunks = ((plane, channels // plane, DH), LOW)
    tiles = ((heads, 3 * half, half), LOW)
    whole = ((rows, channels), WIDE)
    result = ((rows, channels), LOW)

    (own,) = call(own_state_kernel, [chunks], key_vectors, values, flops=unit)
    prefix_low = scan_states(own, place, False)
    probs, intra = call(
        intra_kernel, [tiles, whole], queries, key_vectors, values, flops=6 * unit
    )
    attended, sums = call(
        attend_kernel,
        [whole, ((members, 2 * rows // DH, DH), WIDE)],
        queries, prefix_low, intra, cotangent, gain, flops=unit,
    )
    sums = lax.all_to_all(sums, HEAD, 0, 0)
    grad, own_grad, inverse = call(
        functools.partial(grad_kernel, full_width),
        [result, chunks, ((rows, DH), WIDE)],
        sums, attended, cotangent, gain, queries, flops=unit,
    )
    later_low = scan_states(own_grad, place, True)
    grad_probs, query_grad, normed_out = call(
        query_grad_kernel,
        [tiles, result, result],
        grad, key_vectors, values, prefix_low, attended, inverse, gain, flops=7 * unit,
    )
    key_part, value_part = call(
        partial_kernel, [whole, whole], grad, queries, probs, grad_probs, flops=6 * unit
    )
    key_grad, value_grad = call(
        final_kernel,
        [result, result],
        key_vectors, values, later_low, key_part, value_part, flops=2 * unit,
    )
    return (normed_out, query_grad, key_grad, value_grad)


def solution(mesh):
    fine = Mesh(
        mesh.devices.reshape(8, 4, 2, 4, 2), ("z_lo", "x", "core", "y", "z_hi")
    )
    placed = (P(CTX, HEAD), P(CTX, HEAD), P(CTX, HEAD), P(HEAD), P(CTX, HEAD))
    return jax.shard_map(
        on_device,
        mesh=fine,
        in_specs=placed,
        out_specs=(P(CTX, HEAD),) * 4,
        check_vma=False,
    )
```

time: 144 us -> 116 us (0.81)
  blocking collectives: 0 us -> 62.4 us
  starting transfers between devices: 49.9 us -> 20.3 us
  waiting for transfers between devices: 40.4 us -> 12.4 us
  other arithmetic: 20.9 us -> 0 us
  matrix products: 19.8 us -> 0 us
  Pallas kernels: 0 us -> 9.19 us
    all_to_all x0 -> x4, blocking collectives: none -> 62.4 us  [the longest x2 24.7 us: scan_states(): mine = lax.all_to_all(chunks, PLANE, 0, 0)]
    all_to_all x7 -> x3, starting transfers between devices: 49.9 us -> 20.3 us  [the longest x2 11.7 us: scan_states(): return lax.all_to_all(low, PLANE, 0, 0)]
    all_to_all x7 -> x3, waiting for transfers between devices: 40.4 us -> 12.4 us  [the longest x1 10.3 us: scan_states(): totals = lax.all_to_all(spread, LINE, 0, 0)]
    dot_general x12 -> x0, matrix products: 19.8 us -> none  [the longest x1 2.54 us: on_device(): jnp.einsum('hts,thd->shd', grad_probs, query_heads, preferred_element_typ...]
    unnamed x14 -> x0, other arithmetic: 14 us -> none
    pallas_call x0 -> x11, Pallas kernels: none -> 9.19 us  [call(): pl.pallas_call(kernel, out_shape=outs, in_specs=[IN_SMEM] * scalars + [IN...]
    unnamed x27 -> x34, local copies, waits for them, and re-layouts: 4.97 us -> 10.3 us
    reshape x4 -> x0, local copies, waits for them, and re-layouts: 3.29 us -> none  [the longest x3 2.96 us: split_heads(): return tensor.reshape(row_count, local_heads, DH)]
  transfers between devices with their start and end apart: 7 -> 3, of which waited for: 7 -> 2; matrix products, arithmetic and copies ran while one was open for 10% -> 0% of each run, Pallas kernels for 0% -> 4%
where the time goes in v2:
time: 116 us; the launch traced here: 115 us
  blocking collectives  62.4 us (54%)
  starting transfers between devices  20.3 us (18%)
  waiting for transfers between devices  12.4 us (11%)
  local copies, waits for them, and re-layouts  10.3 us (9%)
  Pallas kernels  9.19 us (8%)
    all_to_all x2, blocking collectives, scan_states(): mine = lax.all_to_all(chunks, PLANE, 0, 0)  24.7 us
    all_to_all x1, blocking collectives, on_device(): sums = lax.all_to_all(sums, HEAD, 0, 0)  23.6 us
    all_to_all x1, blocking collectives, scan_states(): totals = lax.all_to_all(spread, LINE, 0, 0)  14.1 us
    all_to_all x2, starting transfers between devices, scan_states(): return lax.all_to_all(low, PLANE, 0, 0)  11.7 us
    all_to_all x1, waiting for transfers between devices, scan_states(): totals = lax.all_to_all(spread, LINE, 0, 0)  10.3 us
    unnamed x34, local copies, waits for them, and re-layouts  10.3 us
    pallas_call x11, Pallas kernels, call(): pl.pallas_call(kernel, out_shape=outs, in_specs=[IN_SMEM] * scalars + [IN...  9.19 us
    all_to_all x1, starting transfers between devices, scan_states(): totals = lax.all_to_all(spread, LINE, 0, 0)  8.59 us
  transfers between devices with their start and end apart: 3, of which 2 were waited for; matrix products, arithmetic and copies ran while one was open for 0% of the time, Pallas kernels for 4%

profile of v2, /device:TPU:1, one launch (start us, length us, event | category | flops | bytes accessed | tf_op | source)
XLA Modules:
  0.0 115.3 jit_solution(15858686503922873819)
XLA Ops:
  0.6 0.0 copy-start
  0.6 1.0 copy-done
  1.7 0.0 copy-start.2
  1.7 1.0 copy-done.2
  2.7 0.0 copy-start.1
  2.7 0.0 copy-start.3
  2.7 0.0 copy-start.4
  2.7 0.3 shard_map.84
  3.1 0.0 copy-start.5
  3.1 0.0 copy-start.16
  3.1 14.7 %all_to_all.35.mine_ref = bf16[8,64,128]{2,1,0:T(8,128)(2,1)S(1)} all-to-all(bf16[8,64,128]{2,1,0:T(8,128)(2,1)S(1)} %shard_map.84), channel_id=1, replica_groups=mesh['z_lo'=8,'x'=4,'core'=2,'y'=4,'z_hi'=2] {'x','core'}, dimensions={0} | all-to-all | bytes 262144 | tf_op jit(solution)/shard_map/all_to_all | solution.py:222
  17.8 0.7 shard_map.85
  18.4 8.6 %all-to-all-start.1 = ((bf16[8,64,128]{2,1,0:T(8,128)(2,1)}), bf16[8,64,128]{2,1,0:T(8,128)(2,1)S(1)}, u32[]{:S(2)}, u32[]{:S(2)}) async-start(bf16[8,64,128]{2,1,0:T(8,128)(2,1)} %shard_map.85), calls=%async_computation.1 | async-start | bytes 262144 | tf_op jit(solution)/shard_map/all_to_all | solution.py:224
  27.0 10.3 %all-to-all-done.1.totals_ref = bf16[8,64,128]{2,1,0:T(8,128)(2,1)S(1)} async-done(((bf16[8,64,128]{2,1,0:T(8,128)(2,1)}), bf16[8,64,128]{2,1,0:T(8,128)(2,1)S(1)}, u32[]{:S(2)}, u32[]{:S(2)}) %all-to-all-start.1) | async-done | bytes 131104 | tf_op jit(solution)/shard_map/all_to_all | solution.py:224
  37.3 0.7 shard_map.86
  38.0 5.9 %all-to-all-start.2 = ((bf16[8,64,128]{2,1,0:T(8,128)(2,1)}), bf16[8,64,128]{2,1,0:T(8,128)(2,1)S(1)}, u32[]{:S(2)}, u32[]{:S(2)}) async-start(bf16[8,64,128]{2,1,0:T(8,128)(2,1)} %shard_map.86), calls=%async_computation.2 | async-start | bytes 262144 | tf_op jit(solution)/shard_map/all_to_all | solution.py:228
  43.9 0.0 copy-done.1
  43.9 0.0 copy-done.3
  43.9 0.0 copy-done.4
  43.9 1.1 shard_map.87
  45.0 0.0 copy-start.8
  45.0 1.2 %copy-done.8 = bf16[4,768,256]{2,1,0:T(8,128)(2,1)} copy-done((bf16[4,768,256]{2,1,0:T(8,128)(2,1)}, bf16[4,768,256]{2,1,0:T(8,128)(2,1)S(1)}, u32[]{:S(2)}) %copy-start.8) | copy-done | bytes 1572888
  46.2 0.0 copy-start.12
  46.2 1.0 copy-done.12
  47.2 2.0 %all-to-all-done.2.low_ref = bf16[8,64,128]{2,1,0:T(8,128)(2,1)S(1)} async-done(((bf16[8,64,128]{2,1,0:T(8,128)(2,1)}), bf16[8,64,128]{2,1,0:T(8,128)(2,1)S(1)}, u32[]{:S(2)}, u32[]{:S(2)}) %all-to-all-start.2) | async-done | bytes 131104 | tf_op jit(solution)/shard_map/all_to_all | solution.py:228
  49.2 0.0 copy-done.5
  49.2 0.0 copy-done.16
  49.2 1.2 %copy-done.13 = f32[512,512]{1,0:T(8,128)S(1)} copy-done((f32[512,512]{1,0:T(8,128)S(1)}, f32[512,512]{1,0:T(8,128)}, u32[]{:S(2)}) %copy-start.13) | copy-done | bytes 1048600
  50.4 0.5 shard_map.88
  51.0 23.6 %all_to_all.36.sums_ref = f32[8,8,128]{2,1,0:T(8,128)S(1)} all-to-all(f32[8,8,128]{2,1,0:T(8,128)S(1)} %get-tuple-element.19), channel_id=1, replica_groups=mesh['z_lo'=8,'x'=4,'core'=2,'y'=4,'z_hi'=2] {'y','z_hi'}, dimensions={0} | all-to-all | bytes 65536 | tf_op jit(solution)/shard_map/all_to_all | solution.py:256
  74.5 0.6 shard_map.89
  75.1 0.0 copy-start.6
  75.1 0.8 copy-done.6
  75.9 0.7 copy-done.14
  76.6 10.1 %all_to_all.37.mine_ref = bf16[8,64,128]{2,1,0:T(8,128)(2,1)S(1)} all-to-all(bf16[8,64,128]{2,1,0:T(8,128)(2,1)S(1)} %get-tuple-element.25), channel_id=1, replica_groups=mesh['z_lo'=8,'x'=4,'core'=2,'y'=4,'z_hi'=2] {'x','core'}, dimensions={0} | all-to-all | bytes 262144 | tf_op jit(solution)/shard_map/all_to_all | solution.py:222
  86.7 14.1 %all_to_all.38.totals_ref = bf16[8,64,128]{2,1,0:T(8,128)(2,1)S(1)} all-to-all(bf16[8,64,128]{2,1,0:T(8,128)(2,1)S(1)} %shard_map.91), channel_id=1, replica_groups=mesh['z_lo'=8,'x'=4,'core'=2,'y'=4,'z_hi'=2] {'z_lo'}, dimensions={0} | all-to-all | bytes 262144 | tf_op jit(solution)/shard_map/all_to_all | solution.py:224
  100.8 0.7 shard_map.92
  101.5 5.9 %all-to-all-start.6 = ((bf16[8,64,128]{2,1,0:T(8,128)(2,1)}), bf16[8,64,128]{2,1,0:T(8,128)(2,1)S(1)}, u32[]{:S(2)}, u32[]{:S(2)}) async-start(bf16[8,64,128]{2,1,0:T(8,128)(2,1)} %shard_map.92), calls=%async_computation.6 | async-start | bytes 262144 | tf_op jit(solution)/shard_map/all_to_all | solution.py:228
  107.4 0.0 copy-done.7
  107.4 1.1 copy-done.15
  108.5 2.1 %shard_map.90 = (bf16[4,768,256]{2,1,0:T(8,128)(2,1)S(1)}, bf16[512,512]{1,0:T(8,128)(2,1)}, bf16[512,512]{1,0:T(8,128)(2,1)}) custom-call(bf16[512,512]{1,0:T(8,128)(2,1)S(1)} %copy-done.7, bf16[512,512]{1,0:T(8,128)(2,1)S(1)} %copy-done.1, bf16[512,512]{1,0:T(8,128)(2,1)S(1)} %copy-done.3, bf16[8,64,128]{2,1,0:T(8,128)(2,1)S(1)} %all-to-all-done.2.low_ref, ...), custom_call_target="tpu_custom_call" | custom-call | flops 469762048 | bytes 5638144 | tf_op jit(solution)/shard_map/pallas_call | solution.py:209
  110.6 0.0 copy-done.9
  110.6 1.0 shard_map.93
  111.6 0.0 copy-start.10
  111.6 1.0 copy-done.10
  112.6 0.0 all-to-all-done.6.later_ref
  112.7 1.2 %copy-done.11 = f32[512,512]{1,0:T(8,128)S(1)} copy-done((f32[512,512]{1,0:T(8,128)S(1)}, f32[512,512]{1,0:T(8,128)}, u32[]{:S(2)}) %copy-start.11) | copy-done | bytes 1048600
  113.9 1.4 %shard_map.94 = (bf16[512,512]{1,0:T(8,128)(2,1)}, bf16[512,512]{1,0:T(8,128)(2,1)}) custom-call(bf16[512,512]{1,0:T(8,128)(2,1)S(1)} %copy-done.1, bf16[512,512]{1,0:T(8,128)(2,1)S(1)} %copy-done.3, bf16[8,64,128]{2,1,0:T(8,128)(2,1)S(1)} %all-to-all-done.6.later_ref, f32[512,512]{1,0:T(8,128)S(1)} %get-tuple-element.28.key_part_ref, f32[512,512]{1,0:T(8,128)S(1)} %copy-done.11), custom_call_target="tpu_custom_call" | custom-call | flops 134217728 | bytes 4325376 | tf_op jit(solution)/shard_map/pallas_call | solution.py:209
  (7 shorter events, 0.0 us)
Async XLA Ops:
  0.6 1.0 copy-start
  1.7 1.0 copy-start.2
  2.7 41.2 %copy-start.1 = (bf16[512,512]{1,0:T(8,128)(2,1)S(1)}, bf16[512,512]{1,0:T(8,128)(2,1)}, u32[]{:S(2)}) copy-start(bf16[512,512]{1,0:T(8,128)(2,1)} %key_ref.5) | copy-start | bytes 1572868
  2.7 41.2 %copy-start.3 = (bf16[512,512]{1,0:T(8,128)(2,1)S(1)}, bf16[512,512]{1,0:T(8,128)(2,1)}, u32[]{:S(2)}) copy-start(bf16[512,512]{1,0:T(8,128)(2,1)} %value_ref.5) | copy-start | bytes 1572868
  2.7 41.2 %copy-start.4 = (bf16[512,512]{1,0:T(8,128)(2,1)S(1)}, bf16[512,512]{1,0:T(8,128)(2,1)}, u32[]{:S(2)}) copy-start(bf16[512,512]{1,0:T(8,128)(2,1)} %query_ref.7) | copy-start | bytes 1572868
  3.1 46.1 %copy-start.5 = (bf16[512,512]{1,0:T(8,128)(2,1)S(1)}, bf16[512,512]{1,0:T(8,128)(2,1)}, u32[]{:S(2)}) copy-start(bf16[512,512]{1,0:T(8,128)(2,1)} %cotangent_ref.3) | copy-start | bytes 1572868
  3.1 46.1 %copy-start.16 = (f32[512]{0:T(512)S(1)}, f32[512]{0:T(512)}, u32[]{:S(2)}) copy-start(f32[512]{0:T(512)} %param.8) | copy-start | bytes 6148
  18.4 18.9 %all-to-all-start.1 = ((bf16[8,64,128]{2,1,0:T(8,128)(2,1)}), bf16[8,64,128]{2,1,0:T(8,128)(2,1)S(1)}, u32[]{:S(2)}, u32[]{:S(2)}) async-start(bf16[8,64,128]{2,1,0:T(8,128)(2,1)} %shard_map.85), calls=%async_computation.1 | async-start | bytes 262144 | tf_op jit(solution)/shard_map/all_to_all | solution.py:224
  38.0 11.2 %all-to-all-start.2 = ((bf16[8,64,128]{2,1,0:T(8,128)(2,1)}), bf16[8,64,128]{2,1,0:T(8,128)(2,1)S(1)}, u32[]{:S(2)}, u32[]{:S(2)}) async-start(bf16[8,64,128]{2,1,0:T(8,128)(2,1)} %shard_map.86), calls=%async_computation.2 | async-start | bytes 262144 | tf_op jit(solution)/shard_map/all_to_all | solution.py:228
  45.0 1.2 %copy-start.8 = (bf16[4,768,256]{2,1,0:T(8,128)(2,1)}, bf16[4,768,256]{2,1,0:T(8,128)(2,1)S(1)}, u32[]{:S(2)}) copy-start(bf16[4,768,256]{2,1,0:T(8,128)(2,1)S(1)} %get-tuple-element.26.tiles_ref) | copy-start | bytes 4718596
  46.2 1.0 copy-start.12
  49.2 1.2 %copy-start.13 = (f32[512,512]{1,0:T(8,128)S(1)}, f32[512,512]{1,0:T(8,128)}, u32[]{:S(2)}) copy-start(f32[512,512]{1,0:T(8,128)} %copy-done.12) | copy-start | bytes 3145732
  75.1 0.8 copy-start.6
  75.9 0.7 copy-start.14
  76.6 30.8 %copy-start.7 = (bf16[512,512]{1,0:T(8,128)(2,1)S(1)}, bf16[512,512]{1,0:T(8,128)(2,1)}, u32[]{:S(2)}) copy-start(bf16[512,512]{1,0:T(8,128)(2,1)} %copy-done.6) | copy-start | bytes 1572868
  101.5 11.2 %all-to-all-start.6 = ((bf16[8,64,128]{2,1,0:T(8,128)(2,1)}), bf16[8,64,128]{2,1,0:T(8,128)(2,1)S(1)}, u32[]{:S(2)}, u32[]{:S(2)}) async-start(bf16[8,64,128]{2,1,0:T(8,128)(2,1)} %shard_map.92), calls=%async_computation.6 | async-start | bytes 262144 | tf_op jit(solution)/shard_map/all_to_all | solution.py:228
  107.4 3.2 %copy-start.9 = (bf16[4,768,256]{2,1,0:T(8,128)(2,1)S(1)}, bf16[4,768,256]{2,1,0:T(8,128)(2,1)}, u32[]{:S(2)}) copy-start(bf16[4,768,256]{2,1,0:T(8,128)(2,1)} %copy-done.8) | copy-start | bytes 4718596
  107.4 1.1 copy-start.15
  111.6 1.0 copy-start.10
  112.7 1.2 %copy-start.11 = (f32[512,512]{1,0:T(8,128)S(1)}, f32[512,512]{1,0:T(8,128)}, u32[]{:S(2)}) copy-start(f32[512,512]{1,0:T(8,128)} %copy-done.10) | copy-start | bytes 3145732

commit v3 on v2

--- a/solution.py
+++ b/solution.py
@@ -47,10 +47,26 @@
     )
 
 
-def own_state_kernel(left_ref, right_ref, out_ref):
-    for head in range(left_ref.shape[1] // DH):
-        at = head_columns(head)
-        put_state(out_ref, head, dot(left_ref[:, at], right_ref[:, at], 0, 0))
+def own_state_kernel(place_ref, left_hbm, right_hbm, out_ref, left_ref, right_ref, total_ref, sems):
+    rows, channels = left_ref.shape
+    copies = []
+    for block in range(rows // DH):
+        at = pl.ds(block * DH, DH)
+        for side, (source, target) in enumerate(((left_hbm, left_ref), (right_hbm, right_ref))):
+            copies.append(pltpu.make_async_copy(source.at[at], target.at[at], sems.at[side, block]))
+            copies[-1].start()
+    half = rows // 2
+    for part in range(2):
+        for copy in copies[part * len(copies) // 2 : (part + 1) * len(copies) // 2]:
+            copy.wait()
+        at_rows = slice(part * half, (part + 1) * half)
+        for head in range(channels // DH):
+            at = head_columns(head)
+            state = dot(left_ref[at_rows, at], right_ref[at_rows, at], 0, 0)
+            if part == 0:
+                total_ref[head] = state
+            else:
+                put_state(out_ref, head, total_ref[head] + state)
 
 
 def masked_tiles(left_ref, right_ref, at, out_ref, head):
@@ -77,7 +93,7 @@
     return first, last
 
 
-def intra_kernel(query_ref, key_ref, value_ref, tiles_ref, intra_ref):
+def intra_kernel(query_ref, key_ref, value_ref, after_ref, intra_ref, tiles_ref):
     half = query_ref.shape[0] // 2
     for head in range(query_ref.shape[1] // DH):
         at = head_columns(head)
@@ -94,7 +110,8 @@
     out_ref[...] = jnp.broadcast_to(total.astype(LOW)[None], out_ref.shape)
 
 
-def chunks_kernel(backward, place_ref, mine_ref, totals_ref, out_ref):
+def chunks_kernel(backward, place_ref, mine_ref, totals_ref, *rest):
+    out_ref = rest[-1]
     place = place_ref[0]
     running = jnp.zeros(mine_ref.shape[1:], WIDE)
     for plane in range(totals_ref.shape[0]):
@@ -153,28 +170,21 @@
         put_state(own_ref, head, dot(query_ref[:, at], grad_ref[:, at], 0, 0))
 
 
-def query_grad_kernel(
-    grad_ref, key_ref, value_ref, low_ref, attended_ref, inverse_ref, gain_ref,
-    grad_tiles_ref, query_grad_ref, normed_ref,
+def products_kernel(
+    grad_ref, query_ref, key_ref, value_ref, low_ref, attended_ref, inverse_ref, gain_ref, after_ref,
+    query_grad_ref, normed_ref, key_part_ref, value_part_ref, tiles_ref, grad_tiles_ref,
 ):
     half = grad_ref.shape[0] // 2
     inverse = inverse_ref[...]
     for head in range(grad_ref.shape[1] // DH):
         at = head_columns(head)
+        masked_tiles(query_ref, key_ref, at, tiles_ref, head)
         masked_tiles(grad_ref, value_ref, at, grad_tiles_ref, head)
         inter = dot(grad_ref[:, at], state_of(low_ref, head), 1, 1)
         top, bottom = rows_product(grad_tiles_ref, head, key_ref, at)
         query_grad_ref[:half, at] = (top + inter[:half]).astype(LOW)
         query_grad_ref[half:, at] = (bottom + inter[half:]).astype(LOW)
         normed_ref[:, at] = (gain_ref[:, at] * attended_ref[:, at] * inverse).astype(LOW)
-
-
-def partial_kernel(
-    grad_ref, query_ref, tiles_ref, grad_tiles_ref, key_part_ref, value_part_ref
-):
-    half = grad_ref.shape[0] // 2
-    for head in range(grad_ref.shape[1] // DH):
-        at = head_columns(head)
         first, last = columns_product(grad_tiles_ref, head, query_ref, at)
         key_part_ref[:half, at] = first
         key_part_ref[half:, at] = last
@@ -184,24 +194,40 @@
 
 
 def final_kernel(
-    key_ref, value_ref, later_ref, key_part_ref, value_part_ref, key_grad_ref, value_grad_ref
+    key_ref, value_ref, later_ref, key_part_ref, value_part_ref, key_grad_hbm, value_grad_hbm,
+    key_grad_ref, value_grad_ref, sems,
 ):
-    for head in range(key_ref.shape[1] // DH):
-        at = head_columns(head)
-        later = state_of(later_ref, head)
-        key_grad_ref[:, at] = (
-            key_part_ref[:, at] + dot(value_ref[:, at], later, 1, 1)
-        ).astype(LOW)
-        value_grad_ref[:, at] = (
-            value_part_ref[:, at] + dot(key_ref[:, at], later, 1, 0)
-        ).astype(LOW)
+    rows, channels = key_ref.shape
+    copies = []
+    for block in range(rows // DH):
+        at_rows = slice(block * DH, (block + 1) * DH)
+        for head in range(channels // DH):
+            at = head_columns(head)
+            later = state_of(later_ref, head)
+            key_grad_ref[at_rows, at] = (
+                key_part_ref[at_rows, at] + dot(value_ref[at_rows, at], later, 1, 1)
+            ).astype(LOW)
+            value_grad_ref[at_rows, at] = (
+                value_part_ref[at_rows, at] + dot(key_ref[at_rows, at], later, 1, 0)
+            ).astype(LOW)
+        span = pl.ds(block * DH, DH)
+        for side, (source, target) in enumerate(
+            ((key_grad_ref, key_grad_hbm), (value_grad_ref, value_grad_hbm))
+        ):
+            copies.append(pltpu.make_async_copy(source.at[span], target.at[span], sems.at[side, block]))
+            copies[-1].start()
+    for copy in copies:
+        copy.wait()
 
 
 IN_VMEM = pl.BlockSpec(memory_space=pltpu.VMEM)
 IN_SMEM = pl.BlockSpec(memory_space=pltpu.SMEM)
-
-
-def call(kernel, shapes, *operands, flops=0, scalars=0, mib=8):
+ANYWHERE = pl.BlockSpec(memory_space=pl.ANY)
+IN_HBM = pl.BlockSpec(memory_space=pltpu.HBM)
+
+
+def call(kernel, shapes, *operands, flops=0, places="", out_places="", scratch=(), mib=8):
+    kinds = {"v": IN_VMEM, "s": IN_SMEM, "a": ANYWHERE, "h": IN_HBM}
     outs = tuple(jax.ShapeDtypeStruct(shape, kind) for shape, kind in shapes)
     moved = sum(a.size * a.dtype.itemsize for a in operands) + sum(
         o.size * o.dtype.itemsize for o in outs
@@ -209,23 +235,27 @@
     return pl.pallas_call(
         kernel,
         out_shape=outs,
-        in_specs=[IN_SMEM] * scalars + [IN_VMEM] * (len(operands) - scalars),
-        out_specs=tuple(IN_VMEM for _ in outs),
-        compiler_params=pltpu.CompilerParams(vmem_limit_bytes=mib * 2**20),
+        in_specs=[kinds[k] for k in places or "v" * len(operands)],
+        out_specs=tuple(kinds[k] for k in out_places or "v" * len(outs)),
+        scratch_shapes=scratch,
+        compiler_params=pltpu.CompilerParams(vmem_limit_bytes=int(mib * 2**20)),
         cost_estimate=pl.CostEstimate(flops=flops, bytes_accessed=moved, transcendentals=0),
     )(*operands)
 
 
-def scan_states(chunks, place, backward):
+def scan_states(chunks, place, backward, beside=None):
     shape = (chunks.shape, LOW)
     line = lax.axis_size(LINE)
     mine = lax.all_to_all(chunks, PLANE, 0, 0)
     (spread,) = call(totals_kernel, [((line,) + mine.shape[1:], LOW)], mine)
     totals = lax.all_to_all(spread, LINE, 0, 0)
+    extra = () if beside is None else tuple(beside(spread))
+    order = extra[-1:]
     (low,) = call(
-        functools.partial(chunks_kernel, backward), [shape], place, mine, totals, scalars=1
-    )
-    return lax.all_to_all(low, PLANE, 0, 0)
+        functools.partial(chunks_kernel, backward), [shape], place, mine, totals, *order,
+        places="svv" + "a" * len(order),
+    )
+    return low, extra
 
 
 def on_device(queries, key_vectors, values, norm_gain, cotangent):
@@ -239,14 +269,21 @@
     gain = norm_gain.reshape(1, channels)
     unit = 2 * rows * DH * DH * heads
     chunks = ((plane, channels // plane, DH), LOW)
-    tiles = ((heads, 3 * half, half), LOW)
     whole = ((rows, channels), WIDE)
     result = ((rows, channels), LOW)
-
-    (own,) = call(own_state_kernel, [chunks], key_vectors, values, flops=unit)
-    prefix_low = scan_states(own, place, False)
-    probs, intra = call(
-        intra_kernel, [tiles, whole], queries, key_vectors, values, flops=6 * unit
+    buffer = pltpu.VMEM(*result)
+    tiles = pltpu.VMEM((heads, 3 * half, half), LOW)
+    sems = pltpu.SemaphoreType.DMA((2, rows // DH))
+
+    (own,) = call(
+        own_state_kernel, [chunks], place, key_vectors, values, flops=unit, places="shh",
+        scratch=[buffer, buffer, pltpu.VMEM((heads, DH, DH), WIDE), sems], mib=53.6,
+    )
+    low, _ = scan_states(own, place, False)
+    prefix_low = lax.all_to_all(low, PLANE, 0, 0)
+    (intra,) = call(
+        intra_kernel, [whole], queries, key_vectors, values, low, flops=6 * unit,
+        places="vvva", scratch=[tiles],
     )
     attended, sums = call(
         attend_kernel,
@@ -259,19 +296,23 @@
         [result, chunks, ((rows, DH), WIDE)],
         sums, attended, cotangent, gain, queries, flops=unit,
     )
-    later_low = scan_states(own_grad, place, True)
-    grad_probs, query_grad, normed_out = call(
-        query_grad_kernel,
-        [tiles, result, result],
-        grad, key_vectors, values, prefix_low, attended, inverse, gain, flops=7 * unit,
-    )
-    key_part, value_part = call(
-        partial_kernel, [whole, whole], grad, queries, probs, grad_probs, flops=6 * unit
-    )
+
+    def products(after):
+        return call(
+            products_kernel,
+            [result, result, whole, whole],
+            grad, queries, key_vectors, values, prefix_low, attended, inverse, gain, after,
+            flops=16 * unit, places="vvvvvvvva", scratch=[tiles, tiles], mib=10,
+        )
+
+    low, extra = scan_states(own_grad, place, True, products)
+    query_grad, normed_out, key_part, value_part = extra
+    later_low = lax.all_to_all(low, PLANE, 0, 0)
     key_grad, value_grad = call(
         final_kernel,
         [result, result],
         key_vectors, values, later_low, key_part, value_part, flops=2 * unit,
+        out_places="hh", scratch=[buffer, buffer, sems],
     )
     return (normed_out, query_grad, key_grad, value_grad)
 

time: 116 us -> 110 us (0.948)
  blocking collectives: 62.4 us -> 77.2 us
  starting transfers between devices: 20.3 us -> 9.88 us
  local copies, waits for them, and re-layouts: 10.3 us -> 3.28 us
  waiting for transfers between devices: 12.4 us -> 7.81 us
    all_to_all x0 -> x1, blocking collectives: none -> 10.4 us  [on_device(): later_low = lax.all_to_all(low, PLANE, 0, 0)]
    unnamed x34 -> x22, local copies, waits for them, and re-layouts: 10.3 us -> 3.28 us
    all_to_all x1, waiting for transfers between devices: 10.3 us -> 3.65 us  [scan_states(): totals = lax.all_to_all(spread, LINE, 0, 0)]
    all_to_all x2 -> x1, starting transfers between devices: 11.7 us -> 5.86 us  [on_device(): prefix_low = lax.all_to_all(low, PLANE, 0, 0)]
    all_to_all x1, blocking collectives: 14.1 us -> 18.8 us  [scan_states(): totals = lax.all_to_all(spread, LINE, 0, 0)]
    all_to_all x1, starting transfers between devices: 8.59 us -> 4.01 us  [scan_states(): totals = lax.all_to_all(spread, LINE, 0, 0)]
    all_to_all x2 -> x1, waiting for transfers between devices: 2.07 us -> 4.17 us  [on_device(): prefix_low = lax.all_to_all(low, PLANE, 0, 0)]
    pallas_call x11 -> x10, Pallas kernels: 9.19 us -> 10.2 us  [call(): pl.pallas_call(kernel, out_shape=outs, in_specs=[kinds[k] for k in places...]
  transfers between devices with their start and end apart: 3 -> 2, of which waited for: 2 -> 2; matrix products, arithmetic and copies ran while one was open for 0% -> 0% of each run, Pallas kernels for 4% -> 4%
where the time goes in v3:
time: 110 us; the launch traced here: 109 us
  blocking collectives  77.2 us (70%)
  Pallas kernels  10.2 us (9%)
  starting transfers between devices  9.88 us (9%)
  waiting for transfers between devices  7.81 us (7%)
  local copies, waits for them, and re-layouts  3.28 us (3%)
    all_to_all x2, blocking collectives, scan_states(): mine = lax.all_to_all(chunks, PLANE, 0, 0)  24.5 us
    all_to_all x1, blocking collectives, on_device(): sums = lax.all_to_all(sums, HEAD, 0, 0)  23.6 us
    all_to_all x1, blocking collectives, scan_states(): totals = lax.all_to_all(spread, LINE, 0, 0)  18.8 us
    all_to_all x1, blocking collectives, on_device(): later_low = lax.all_to_all(low, PLANE, 0, 0)  10.4 us
    pallas_call x10, Pallas kernels, call(): pl.pallas_call(kernel, out_shape=outs, in_specs=[kinds[k] for k in places...  10.2 us
    all_to_all x1, starting transfers between devices, on_device(): prefix_low = lax.all_to_all(low, PLANE, 0, 0)  5.86 us
    all_to_all x1, waiting for transfers between devices, on_device(): prefix_low = lax.all_to_all(low, PLANE, 0, 0)  4.17 us
    all_to_all x1, starting transfers between devices, scan_states(): totals = lax.all_to_all(spread, LINE, 0, 0)  4.01 us
  transfers between devices with their start and end apart: 2, of which 2 were waited for; matrix products, arithmetic and copies ran while one was open for 0% of the time, Pallas kernels for 4%

profile of v3, /device:TPU:1, one launch (start us, length us, event | category | flops | bytes accessed | tf_op | source)
XLA Modules:
  0.0 109.1 jit_solution(13102993738218426841)
XLA Ops:
  0.6 0.0 copy-start.2
  0.6 1.8 %shard_map.84 = bf16[8,64,128]{2,1,0:T(8,128)(2,1)S(1)} custom-call(s32[1]{0:T(128)} %bitcast.place_ref, bf16[512,512]{1,0:T(8,128)(2,1)} %key_ref.5, bf16[512,512]{1,0:T(8,128)(2,1)} %value_ref.5), custom_call_target="tpu_custom_call" | custom-call | flops 67108864 | bytes 1179652 | tf_op jit(solution)/shard_map/pallas_call | solution.py:235
  2.4 14.5 %all_to_all.35.mine_ref = bf16[8,64,128]{2,1,0:T(8,128)(2,1)S(1)} all-to-all(bf16[8,64,128]{2,1,0:T(8,128)(2,1)S(1)} %shard_map.84), channel_id=1, replica_groups=mesh['z_lo'=8,'x'=4,'core'=2,'y'=4,'z_hi'=2] {'x','core'}, dimensions={0} | all-to-all | bytes 262144 | tf_op jit(solution)/shard_map/all_to_all | solution.py:249
  17.0 0.0 copy-start.1
  17.0 0.0 copy-start
  17.0 18.8 %all_to_all.36.totals_ref = bf16[8,64,128]{2,1,0:T(8,128)(2,1)S(1)} all-to-all(bf16[8,64,128]{2,1,0:T(8,128)(2,1)S(1)} %shard_map.85), channel_id=1, replica_groups=mesh['z_lo'=8,'x'=4,'core'=2,'y'=4,'z_hi'=2] {'z_lo'}, dimensions={0} | all-to-all | bytes 262144 | tf_op jit(solution)/shard_map/all_to_all | solution.py:251
  35.8 0.7 shard_map.86.after_ref
  36.5 5.9 %all-to-all-start.2 = ((bf16[8,64,128]{2,1,0:T(8,128)(2,1)}), bf16[8,64,128]{2,1,0:T(8,128)(2,1)S(1)}, u32[]{:S(2)}, u32[]{:S(2)}) async-start(bf16[8,64,128]{2,1,0:T(8,128)(2,1)} %shard_map.86.after_ref), calls=%async_computation.2 | async-start | bytes 262144 | tf_op jit(solution)/shard_map/all_to_all | solution.py:283
  42.4 0.0 copy-done.2
  42.4 0.0 copy-done.1
  42.4 0.0 copy-done
  42.4 0.0 copy-start.3
  42.4 0.0 copy-start.8
  42.4 1.1 shard_map.87.intra_ref
  43.5 4.2 %all-to-all-done.2.low_ref = bf16[8,64,128]{2,1,0:T(8,128)(2,1)S(1)} async-done(((bf16[8,64,128]{2,1,0:T(8,128)(2,1)}), bf16[8,64,128]{2,1,0:T(8,128)(2,1)S(1)}, u32[]{:S(2)}, u32[]{:S(2)}) %all-to-all-start.2) | async-done | bytes 131104 | tf_op jit(solution)/shard_map/all_to_all | solution.py:283
  47.7 0.0 copy-done.3
  47.7 0.0 copy-done.8
  47.7 0.5 shard_map.88
  48.2 0.0 copy-start.6
  48.2 23.6 %all_to_all.37.sums_ref = f32[8,8,128]{2,1,0:T(8,128)S(1)} all-to-all(f32[8,8,128]{2,1,0:T(8,128)S(1)} %get-tuple-element.15), channel_id=1, replica_groups=mesh['z_lo'=8,'x'=4,'core'=2,'y'=4,'z_hi'=2] {'y','z_hi'}, dimensions={0} | all-to-all | bytes 65536 | tf_op jit(solution)/shard_map/all_to_all | solution.py:293
  71.8 0.6 shard_map.89
  72.3 0.0 copy-done.6
  72.4 0.0 copy-start.9
  72.4 10.0 %all_to_all.38.mine_ref = bf16[8,64,128]{2,1,0:T(8,128)(2,1)S(1)} all-to-all(bf16[8,64,128]{2,1,0:T(8,128)(2,1)S(1)} %get-tuple-element.19), channel_id=1, replica_groups=mesh['z_lo'=8,'x'=4,'core'=2,'y'=4,'z_hi'=2] {'x','core'}, dimensions={0} | all-to-all | bytes 262144 | tf_op jit(solution)/shard_map/all_to_all | solution.py:249
  82.3 0.7 shard_map.90.after_ref
  83.0 4.0 %all-to-all-start.5 = ((bf16[8,64,128]{2,1,0:T(8,128)(2,1)}), bf16[8,64,128]{2,1,0:T(8,128)(2,1)S(1)}, u32[]{:S(2)}, u32[]{:S(2)}) async-start(bf16[8,64,128]{2,1,0:T(8,128)(2,1)} %shard_map.90.after_ref), calls=%async_computation.5 | async-start | bytes 262144 | tf_op jit(solution)/shard_map/all_to_all | solution.py:251
  87.0 0.0 copy-done.9
  87.0 0.0 copy-start.7
  87.0 1.2 %copy-done.7 = f32[512,512]{1,0:T(8,128)S(1)} copy-done((f32[512,512]{1,0:T(8,128)S(1)}, f32[512,512]{1,0:T(8,128)}, u32[]{:S(2)}) %copy-start.7) | copy-done | bytes 1048600
  88.2 0.0 copy-start.10
  88.2 1.0 copy-done.10
  89.3 3.4 %shard_map.91 = (bf16[512,512]{1,0:T(8,128)(2,1)}, bf16[512,512]{1,0:T(8,128)(2,1)}, f32[512,512]{1,0:T(8,128)S(1)}, f32[512,512]{1,0:T(8,128)S(1)}) custom-call(bf16[512,512]{1,0:T(8,128)(2,1)S(1)} %copy-done.10, bf16[512,512]{1,0:T(8,128)(2,1)S(1)} %copy-done, bf16[512,512]{1,0:T(8,128)(2,1)S(1)} %copy-done.1, bf16[512,512]{1,0:T(8,128)(2,1)S(1)} %copy-done.2, ...), custom_call_target="tpu_custom_call" | custom-call | flops 1073741824 | bytes 6817792 | tf_op jit(solution)/shard_map/pallas_call | solution.py:235
  92.7 0.0 copy-start.4
  92.7 1.0 copy-done.4
  93.7 3.6 %all-to-all-done.5.totals_ref = bf16[8,64,128]{2,1,0:T(8,128)(2,1)S(1)} async-done(((bf16[8,64,128]{2,1,0:T(8,128)(2,1)}), bf16[8,64,128]{2,1,0:T(8,128)(2,1)S(1)}, u32[]{:S(2)}, u32[]{:S(2)}) %all-to-all-start.5) | async-done | bytes 131104 | tf_op jit(solution)/shard_map/all_to_all | solution.py:251
  97.3 0.0 copy-start.5
  97.4 10.4 %all_to_all.39.later_ref = bf16[8,64,128]{2,1,0:T(8,128)(2,1)S(1)} all-to-all(bf16[8,64,128]{2,1,0:T(8,128)(2,1)S(1)} %shard_map.92), channel_id=1, replica_groups=mesh['z_lo'=8,'x'=4,'core'=2,'y'=4,'z_hi'=2] {'x','core'}, dimensions={0} | all-to-all | bytes 262144 | tf_op jit(solution)/shard_map/all_to_all | solution.py:310
  107.7 0.0 copy-done.5
  107.8 1.4 %shard_map.93 = (bf16[512,512]{1,0:T(8,128)(2,1)}, bf16[512,512]{1,0:T(8,128)(2,1)}) custom-call(bf16[512,512]{1,0:T(8,128)(2,1)S(1)} %copy-done.1, bf16[512,512]{1,0:T(8,128)(2,1)S(1)} %copy-done.2, bf16[8,64,128]{2,1,0:T(8,128)(2,1)S(1)} %all_to_all.39.later_ref, f32[512,512]{1,0:T(8,128)S(1)} %copy-done.5, ...), custom_call_target="tpu_custom_call" | custom-call | flops 134217728 | bytes 4325376 | tf_op jit(solution)/shard_map/pallas_call | solution.py:235
  (2 shorter events, 0.1 us)
Async XLA Ops:
  0.6 41.8 %copy-start.2 = (bf16[512,512]{1,0:T(8,128)(2,1)S(1)}, bf16[512,512]{1,0:T(8,128)(2,1)}, u32[]{:S(2)}) copy-start(bf16[512,512]{1,0:T(8,128)(2,1)} %value_ref.5) | copy-start | bytes 1572868
  17.0 25.4 %copy-start.1 = (bf16[512,512]{1,0:T(8,128)(2,1)S(1)}, bf16[512,512]{1,0:T(8,128)(2,1)}, u32[]{:S(2)}) copy-start(bf16[512,512]{1,0:T(8,128)(2,1)} %key_ref.5) | copy-start | bytes 1572868
  17.0 25.4 %copy-start = (bf16[512,512]{1,0:T(8,128)(2,1)S(1)}, bf16[512,512]{1,0:T(8,128)(2,1)}, u32[]{:S(2)}) copy-start(bf16[512,512]{1,0:T(8,128)(2,1)} %query_ref.7) | copy-start | bytes 1572868
  36.5 11.2 %all-to-all-start.2 = ((bf16[8,64,128]{2,1,0:T(8,128)(2,1)}), bf16[8,64,128]{2,1,0:T(8,128)(2,1)S(1)}, u32[]{:S(2)}, u32[]{:S(2)}) async-start(bf16[8,64,128]{2,1,0:T(8,128)(2,1)} %shard_map.86.after_ref), calls=%async_computation.2 | async-start | bytes 262144 | tf_op jit(solution)/shard_map/all_to_all | solution.py:283
  42.4 5.3 %copy-start.3 = (bf16[512,512]{1,0:T(8,128)(2,1)S(1)}, bf16[512,512]{1,0:T(8,128)(2,1)}, u32[]{:S(2)}) copy-start(bf16[512,512]{1,0:T(8,128)(2,1)} %cotangent_ref.3) | copy-start | bytes 1572868
  42.4 5.3 %copy-start.8 = (f32[512]{0:T(512)S(1)}, f32[512]{0:T(512)}, u32[]{:S(2)}) copy-start(f32[512]{0:T(512)} %param.8) | copy-start | bytes 6148
  48.2 24.1 %copy-start.6 = (f32[512,512]{1,0:T(8,128)}, f32[512,512]{1,0:T(8,128)S(1)}, u32[]{:S(2)}) copy-start(f32[512,512]{1,0:T(8,128)S(1)} %get-tuple-element.16.attended_ref) | copy-start | bytes 3145732
  72.4 14.7 %copy-start.9 = (bf16[512,512]{1,0:T(8,128)(2,1)}, bf16[512,512]{1,0:T(8,128)(2,1)S(1)}, u32[]{:S(2)}) copy-start(bf16[512,512]{1,0:T(8,128)(2,1)S(1)} %get-tuple-element.17.grad_ref) | copy-start | bytes 1572868
  83.0 14.3 %all-to-all-start.5 = ((bf16[8,64,128]{2,1,0:T(8,128)(2,1)}), bf16[8,64,128]{2,1,0:T(8,128)(2,1)S(1)}, u32[]{:S(2)}, u32[]{:S(2)}) async-start(bf16[8,64,128]{2,1,0:T(8,128)(2,1)} %shard_map.90.after_ref), calls=%async_computation.5 | async-start | bytes 262144 | tf_op jit(solution)/shard_map/all_to_all | solution.py:251
  87.0 1.2 %copy-start.7 = (f32[512,512]{1,0:T(8,128)S(1)}, f32[512,512]{1,0:T(8,128)}, u32[]{:S(2)}) copy-start(f32[512,512]{1,0:T(8,128)} %copy-done.6) | copy-start | bytes 3145732
  88.2 1.0 copy-start.10
  92.7 1.0 copy-start.4
  97.3 10.4 %copy-start.5 = (f32[512,512]{1,0:T(8,128)S(1)}, f32[512,512]{1,0:T(8,128)}, u32[]{:S(2)}) copy-start(f32[512,512]{1,0:T(8,128)} %copy-done.4) | copy-start | bytes 3145732

commit v4 on v3

--- a/solution.py
+++ b/solution.py
@@ -13,6 +13,9 @@
 LINE = "z_lo"
 CTX = ("z_lo", "x", "core")
 HEAD = ("y", "z_hi")
+LINE_ORDER = [7, 6, 5, 4, 3, 2, 1, 0]
+PLANE_ORDER = [4, 5, 6, 7, 0, 1, 2, 3]
+HEAD_ORDER = [5, 7, 1, 3, 4, 6, 0, 2]
 LOW = jnp.bfloat16
 WIDE = jnp.float32
 
@@ -114,13 +117,14 @@
     out_ref = rest[-1]
     place = place_ref[0]
     running = jnp.zeros(mine_ref.shape[1:], WIDE)
-    for plane in range(totals_ref.shape[0]):
+    for slot, plane in enumerate(LINE_ORDER):
         keep = plane > place if backward else plane < place
-        running = running + jnp.where(keep, totals_ref[plane].astype(WIDE), 0.0)
+        running = running + jnp.where(keep, totals_ref[slot].astype(WIDE), 0.0)
     members = mine_ref.shape[0]
     for member in range(members - 1, -1, -1) if backward else range(members):
-        out_ref[member] = running.astype(LOW)
-        running = running + mine_ref[member].astype(WIDE)
+        slot = PLANE_ORDER.index(member)
+        out_ref[slot] = running.astype(LOW)
+        running = running + mine_ref[slot].astype(WIDE)
 
 
 def attend_kernel(query_ref, low_ref, intra_ref, cotangent_ref, gain_ref, attended_ref, sums_ref):
@@ -243,12 +247,16 @@
     )(*operands)
 
 
+def exchange(blocks, axes, order):
+    return lax.all_to_all(blocks, axes, 0, 0, axis_index_groups=[order])
+
+
 def scan_states(chunks, place, backward, beside=None):
     shape = (chunks.shape, LOW)
     line = lax.axis_size(LINE)
-    mine = lax.all_to_all(chunks, PLANE, 0, 0)
+    mine = exchange(chunks, PLANE, PLANE_ORDER)
     (spread,) = call(totals_kernel, [((line,) + mine.shape[1:], LOW)], mine)
-    totals = lax.all_to_all(spread, LINE, 0, 0)
+    totals = exchange(spread, LINE, LINE_ORDER)
     extra = () if beside is None else tuple(beside(spread))
     order = extra[-1:]
     (low,) = call(
@@ -280,7 +288,7 @@
         scratch=[buffer, buffer, pltpu.VMEM((heads, DH, DH), WIDE), sems], mib=53.6,
     )
     low, _ = scan_states(own, place, False)
-    prefix_low = lax.all_to_all(low, PLANE, 0, 0)
+    prefix_low = exchange(low, PLANE, PLANE_ORDER)
     (intra,) = call(
         intra_kernel, [whole], queries, key_vectors, values, low, flops=6 * unit,
         places="vvva", scratch=[tiles],
@@ -290,7 +298,7 @@
         [whole, ((members, 2 * rows // DH, DH), WIDE)],
         queries, prefix_low, intra, cotangent, gain, flops=unit,
     )
-    sums = lax.all_to_all(sums, HEAD, 0, 0)
+    sums = exchange(sums, HEAD, HEAD_ORDER)
     grad, own_grad, inverse = call(
         functools.partial(grad_kernel, full_width),
         [result, chunks, ((rows, DH), WIDE)],
@@ -307,7 +315,7 @@
 
     low, extra = scan_states(own_grad, place, True, products)
     query_grad, normed_out, key_part, value_part = extra
-    later_low = lax.all_to_all(low, PLANE, 0, 0)
+    later_low = exchange(low, PLANE, PLANE_ORDER)
     key_grad, value_grad = call(
         final_kernel,
         [result, result],

time: 110 us -> 97.1 us (0.88)
  blocking collectives: 77.2 us -> 64.5 us
  starting transfers between devices: 9.88 us -> 16.3 us
  waiting for transfers between devices: 7.81 us -> 1.42 us
    all_to_all x5, blocking collectives: 77.2 us -> 64.5 us  [exchange(): return lax.all_to_all(blocks, axes, 0, 0, axis_index_groups=[order])]
    all_to_all x2, starting transfers between devices: 9.88 us -> 16.3 us  [exchange(): return lax.all_to_all(blocks, axes, 0, 0, axis_index_groups=[order])]
    all_to_all x2, waiting for transfers between devices: 7.81 us -> 1.42 us  [exchange(): return lax.all_to_all(blocks, axes, 0, 0, axis_index_groups=[order])]
  transfers between devices with their start and end apart: 2 -> 2, of which waited for: 2 -> 1; matrix products, arithmetic and copies ran while one was open for 0% -> 0% of each run, Pallas kernels for 4% -> 5%
where the time goes in v4:
time: 97.1 us; the launch traced here: 96.5 us
  blocking collectives  64.5 us (66%)
  starting transfers between devices  16.3 us (17%)
  Pallas kernels  10.2 us (11%)
  local copies, waits for them, and re-layouts  3.29 us (3%)
  waiting for transfers between devices  1.42 us (1%)
    all_to_all x5, blocking collectives, exchange(): return lax.all_to_all(blocks, axes, 0, 0, axis_index_groups=[order])  64.5 us
    all_to_all x2, starting transfers between devices, exchange(): return lax.all_to_all(blocks, axes, 0, 0, axis_index_groups=[order])  16.3 us
    pallas_call x10, Pallas kernels, call(): pl.pallas_call(kernel, out_shape=outs, in_specs=[kinds[k] for k in places...  10.2 us
    unnamed x22, local copies, waits for them, and re-layouts  3.29 us
  transfers between devices with their start and end apart: 2, of which 1 were waited for; matrix products, arithmetic and copies ran while one was open for 0% of the time, Pallas kernels for 5%

profile of v4, /device:TPU:1, one launch (start us, length us, event | category | flops | bytes accessed | tf_op | source)
XLA Modules:
  0.0 96.5 jit_solution(7734195338640610762)
XLA Ops:
  0.6 0.0 copy-start.2
  0.6 1.8 %shard_map.84 = bf16[8,64,128]{2,1,0:T(8,128)(2,1)S(1)} custom-call(s32[1]{0:T(128)} %bitcast.place_ref, bf16[512,512]{1,0:T(8,128)(2,1)} %key_ref.5, bf16[512,512]{1,0:T(8,128)(2,1)} %value_ref.5), custom_call_target="tpu_custom_call" | custom-call | flops 67108864 | bytes 1179652 | tf_op jit(solution)/shard_map/pallas_call | solution.py:239
  2.4 13.7 %all_to_all.35.mine_ref = bf16[8,64,128]{2,1,0:T(8,128)(2,1)S(1)} all-to-all(bf16[8,64,128]{2,1,0:T(8,128)(2,1)S(1)} %shard_map.84), channel_id=1, replica_groups={{32,40,48,56,0,8,16,24},{33,41,49,57,1,9,17,25},{34,42,50,58,2,10,18,26..., dimensions={0} | all-to-all | bytes 262144 | tf_op jit(solution)/shard_map/all_to_all | solution.py:251
  16.1 0.0 copy-start.1
  16.1 0.0 copy-start
  16.1 15.8 %all_to_all.36.totals_ref = bf16[8,64,128]{2,1,0:T(8,128)(2,1)S(1)} all-to-all(bf16[8,64,128]{2,1,0:T(8,128)(2,1)S(1)} %shard_map.85), channel_id=1, replica_groups={{448,384,320,256,192,128,64,0},{449,385,321,257,193,129,65,1},{450,386,..., dimensions={0} | all-to-all | bytes 262144 | tf_op jit(solution)/shard_map/all_to_all | solution.py:251
  32.0 0.7 shard_map.86.after_ref
  32.7 7.0 %all-to-all-start.2 = ((bf16[8,64,128]{2,1,0:T(8,128)(2,1)}), bf16[8,64,128]{2,1,0:T(8,128)(2,1)S(1)}, u32[]{:S(2)}, u32[]{:S(2)}) async-start(bf16[8,64,128]{2,1,0:T(8,128)(2,1)} %shard_map.86.after_ref), calls=%async_computation.2 | async-start | bytes 262144 | tf_op jit(solution)/shard_map/all_to_all | solution.py:251
  39.7 0.0 copy-done.2
  39.7 0.0 copy-done.1
  39.7 0.0 copy-done
  39.7 0.0 copy-start.3
  39.7 0.0 copy-start.8
  39.7 1.1 %shard_map.87.intra_ref = f32[512,512]{1,0:T(8,128)S(1)} custom-call(bf16[512,512]{1,0:T(8,128)(2,1)S(1)} %copy-done, bf16[512,512]{1,0:T(8,128)(2,1)S(1)} %copy-done.1, bf16[512,512]{1,0:T(8,128)(2,1)S(1)} %copy-done.2, bf16[8,64,128]{2,1,0:T(8,128)(2,1)} %shard_map.86.after_ref), custom_call_target="tpu_custom_call" | custom-call | flops 402653184 | bytes 2752512 | tf_op jit(solution)/shard_map/pallas_call | solution.py:239
  40.8 1.4 %all-to-all-done.2.low_ref = bf16[8,64,128]{2,1,0:T(8,128)(2,1)S(1)} async-done(((bf16[8,64,128]{2,1,0:T(8,128)(2,1)}), bf16[8,64,128]{2,1,0:T(8,128)(2,1)S(1)}, u32[]{:S(2)}, u32[]{:S(2)}) %all-to-all-start.2) | async-done | bytes 131104 | tf_op jit(solution)/shard_map/all_to_all | solution.py:251
  42.2 0.0 copy-done.3
  42.2 0.0 copy-done.8
  42.3 0.5 shard_map.88
  42.8 0.0 copy-start.6
  42.8 16.1 %all_to_all.37.sums_ref = f32[8,8,128]{2,1,0:T(8,128)S(1)} all-to-all(f32[8,8,128]{2,1,0:T(8,128)S(1)} %get-tuple-element.15), channel_id=1, replica_groups={{5,7,1,3,4,6,0,2},{13,15,9,11,12,14,8,10},{21,23,17,19,20,22,16,18},{29..., dimensions={0} | all-to-all | bytes 65536 | tf_op jit(solution)/shard_map/all_to_all | solution.py:251
  58.9 0.6 shard_map.89
  59.5 0.0 copy-done.6
  59.5 0.0 copy-start.9
  59.5 9.7 %all_to_all.38.mine_ref = bf16[8,64,128]{2,1,0:T(8,128)(2,1)S(1)} all-to-all(bf16[8,64,128]{2,1,0:T(8,128)(2,1)S(1)} %get-tuple-element.19), channel_id=1, replica_groups={{32,40,48,56,0,8,16,24},{33,41,49,57,1,9,17,25},{34,42,50,58,2,10,18,26..., dimensions={0} | all-to-all | bytes 262144 | tf_op jit(solution)/shard_map/all_to_all | solution.py:251
  69.2 0.7 shard_map.90.after_ref
  69.9 9.3 %all-to-all-start.5 = ((bf16[8,64,128]{2,1,0:T(8,128)(2,1)}), bf16[8,64,128]{2,1,0:T(8,128)(2,1)S(1)}, u32[]{:S(2)}, u32[]{:S(2)}) async-start(bf16[8,64,128]{2,1,0:T(8,128)(2,1)} %shard_map.90.after_ref), calls=%async_computation.5 | async-start | bytes 262144 | tf_op jit(solution)/shard_map/all_to_all | solution.py:251
  79.2 0.0 copy-done.9
  79.2 0.0 copy-start.7
  79.2 1.2 %copy-done.7 = f32[512,512]{1,0:T(8,128)S(1)} copy-done((f32[512,512]{1,0:T(8,128)S(1)}, f32[512,512]{1,0:T(8,128)}, u32[]{:S(2)}) %copy-start.7) | copy-done | bytes 1048600
  80.4 0.0 copy-start.10
  80.4 1.0 %copy-done.10 = bf16[512,512]{1,0:T(8,128)(2,1)S(1)} copy-done((bf16[512,512]{1,0:T(8,128)(2,1)S(1)}, bf16[512,512]{1,0:T(8,128)(2,1)}, u32[]{:S(2)}) %copy-start.10) | copy-done | bytes 524312
  81.5 3.4 %shard_map.91 = (bf16[512,512]{1,0:T(8,128)(2,1)}, bf16[512,512]{1,0:T(8,128)(2,1)}, f32[512,512]{1,0:T(8,128)S(1)}, f32[512,512]{1,0:T(8,128)S(1)}) custom-call(bf16[512,512]{1,0:T(8,128)(2,1)S(1)} %copy-done.10, bf16[512,512]{1,0:T(8,128)(2,1)S(1)} %copy-done, bf16[512,512]{1,0:T(8,128)(2,1)S(1)} %copy-done.1, bf16[512,512]{1,0:T(8,128)(2,1)S(1)} %copy-done.2, ...), custom_call_target="tpu_custom_call" | custom-call | flops 1073741824 | bytes 6817792 | tf_op jit(solution)/shard_map/pallas_call | solution.py:239
  84.9 0.0 copy-start.4
  84.9 1.0 %copy-done.4 = f32[512,512]{1,0:T(8,128)} copy-done((f32[512,512]{1,0:T(8,128)}, f32[512,512]{1,0:T(8,128)S(1)}, u32[]{:S(2)}) %copy-start.4) | copy-done | bytes 1048600
  85.9 0.0 all-to-all-done.5.totals_ref
  85.9 0.0 copy-start.5
  85.9 9.2 %all_to_all.39.later_ref = bf16[8,64,128]{2,1,0:T(8,128)(2,1)S(1)} all-to-all(bf16[8,64,128]{2,1,0:T(8,128)(2,1)S(1)} %shard_map.92), channel_id=1, replica_groups={{32,40,48,56,0,8,16,24},{33,41,49,57,1,9,17,25},{34,42,50,58,2,10,18,26..., dimensions={0} | all-to-all | bytes 262144 | tf_op jit(solution)/shard_map/all_to_all | solution.py:251
  95.1 0.0 copy-done.5
  95.1 1.4 %shard_map.93 = (bf16[512,512]{1,0:T(8,128)(2,1)}, bf16[512,512]{1,0:T(8,128)(2,1)}) custom-call(bf16[512,512]{1,0:T(8,128)(2,1)S(1)} %copy-done.1, bf16[512,512]{1,0:T(8,128)(2,1)S(1)} %copy-done.2, bf16[8,64,128]{2,1,0:T(8,128)(2,1)S(1)} %all_to_all.39.later_ref, f32[512,512]{1,0:T(8,128)S(1)} %copy-done.5, ...), custom_call_target="tpu_custom_call" | custom-call | flops 134217728 | bytes 4325376 | tf_op jit(solution)/shard_map/pallas_call | solution.py:239
  (2 shorter events, 0.1 us)
Async XLA Ops:
  0.6 39.1 %copy-start.2 = (bf16[512,512]{1,0:T(8,128)(2,1)S(1)}, bf16[512,512]{1,0:T(8,128)(2,1)}, u32[]{:S(2)}) copy-start(bf16[512,512]{1,0:T(8,128)(2,1)} %value_ref.5) | copy-start | bytes 1572868
  16.1 23.6 %copy-start.1 = (bf16[512,512]{1,0:T(8,128)(2,1)S(1)}, bf16[512,512]{1,0:T(8,128)(2,1)}, u32[]{:S(2)}) copy-start(bf16[512,512]{1,0:T(8,128)(2,1)} %key_ref.5) | copy-start | bytes 1572868
  16.1 23.6 %copy-start = (bf16[512,512]{1,0:T(8,128)(2,1)S(1)}, bf16[512,512]{1,0:T(8,128)(2,1)}, u32[]{:S(2)}) copy-start(bf16[512,512]{1,0:T(8,128)(2,1)} %query_ref.7) | copy-start | bytes 1572868
  32.7 9.6 %all-to-all-start.2 = ((bf16[8,64,128]{2,1,0:T(8,128)(2,1)}), bf16[8,64,128]{2,1,0:T(8,128)(2,1)S(1)}, u32[]{:S(2)}, u32[]{:S(2)}) async-start(bf16[8,64,128]{2,1,0:T(8,128)(2,1)} %shard_map.86.after_ref), calls=%async_computation.2 | async-start | bytes 262144 | tf_op jit(solution)/shard_map/all_to_all | solution.py:251
  39.7 2.5 %copy-start.3 = (bf16[512,512]{1,0:T(8,128)(2,1)S(1)}, bf16[512,512]{1,0:T(8,128)(2,1)}, u32[]{:S(2)}) copy-start(bf16[512,512]{1,0:T(8,128)(2,1)} %cotangent_ref.3) | copy-start | bytes 1572868
  39.7 2.5 %copy-start.8 = (f32[512]{0:T(512)S(1)}, f32[512]{0:T(512)}, u32[]{:S(2)}) copy-start(f32[512]{0:T(512)} %param.8) | copy-start | bytes 6148
  42.8 16.7 %copy-start.6 = (f32[512,512]{1,0:T(8,128)}, f32[512,512]{1,0:T(8,128)S(1)}, u32[]{:S(2)}) copy-start(f32[512,512]{1,0:T(8,128)S(1)} %get-tuple-element.16.attended_ref) | copy-start | bytes 3145732
  59.5 19.7 %copy-start.9 = (bf16[512,512]{1,0:T(8,128)(2,1)}, bf16[512,512]{1,0:T(8,128)(2,1)S(1)}, u32[]{:S(2)}) copy-start(bf16[512,512]{1,0:T(8,128)(2,1)S(1)} %get-tuple-element.17.grad_ref) | copy-start | bytes 1572868
  69.9 16.0 %all-to-all-start.5 = ((bf16[8,64,128]{2,1,0:T(8,128)(2,1)}), bf16[8,64,128]{2,1,0:T(8,128)(2,1)S(1)}, u32[]{:S(2)}, u32[]{:S(2)}) async-start(bf16[8,64,128]{2,1,0:T(8,128)(2,1)} %shard_map.90.after_ref), calls=%async_computation.5 | async-start | bytes 262144 | tf_op jit(solution)/shard_map/all_to_all | solution.py:251
  79.2 1.2 %copy-start.7 = (f32[512,512]{1,0:T(8,128)S(1)}, f32[512,512]{1,0:T(8,128)}, u32[]{:S(2)}) copy-start(f32[512,512]{1,0:T(8,128)} %copy-done.6) | copy-start | bytes 3145732
  80.4 1.0 %copy-start.10 = (bf16[512,512]{1,0:T(8,128)(2,1)S(1)}, bf16[512,512]{1,0:T(8,128)(2,1)}, u32[]{:S(2)}) copy-start(bf16[512,512]{1,0:T(8,128)(2,1)} %copy-done.9) | copy-start | bytes 1572868
  84.9 1.0 %copy-start.4 = (f32[512,512]{1,0:T(8,128)}, f32[512,512]{1,0:T(8,128)S(1)}, u32[]{:S(2)}) copy-start(f32[512,512]{1,0:T(8,128)S(1)} %get-tuple-element.23.key_part_ref) | copy-start | bytes 3145732
  85.9 9.3 %copy-start.5 = (f32[512,512]{1,0:T(8,128)S(1)}, f32[512,512]{1,0:T(8,128)}, u32[]{:S(2)}) copy-start(f32[512,512]{1,0:T(8,128)} %copy-done.4) | copy-start | bytes 3145732

commit v5 on v4

--- a/solution.py
+++ b/solution.py
@@ -14,6 +14,7 @@
 CTX = ("z_lo", "x", "core")
 HEAD = ("y", "z_hi")
 LINE_ORDER = [7, 6, 5, 4, 3, 2, 1, 0]
+LINE_BACK_ORDER = [4, 3, 5, 2, 6, 1, 7, 0]
 PLANE_ORDER = [4, 5, 6, 7, 0, 1, 2, 3]
 HEAD_ORDER = [5, 7, 1, 3, 4, 6, 0, 2]
 LOW = jnp.bfloat16
@@ -96,16 +97,6 @@
     return first, last
 
 
-def intra_kernel(query_ref, key_ref, value_ref, after_ref, intra_ref, tiles_ref):
-    half = query_ref.shape[0] // 2
-    for head in range(query_ref.shape[1] // DH):
-        at = head_columns(head)
-        masked_tiles(query_ref, key_ref, at, tiles_ref, head)
-        top, bottom = rows_product(tiles_ref, head, value_ref, at)
-        intra_ref[:half, at] = top
-        intra_ref[half:, at] = bottom
-
-
 def totals_kernel(mine_ref, out_ref):
     total = mine_ref[0].astype(WIDE)
     for member in range(1, mine_ref.shape[0]):
@@ -117,7 +108,7 @@
     out_ref = rest[-1]
     place = place_ref[0]
     running = jnp.zeros(mine_ref.shape[1:], WIDE)
-    for slot, plane in enumerate(LINE_ORDER):
+    for slot, plane in enumerate(LINE_BACK_ORDER if backward else LINE_ORDER):
         keep = plane > place if backward else plane < place
         running = running + jnp.where(keep, totals_ref[slot].astype(WIDE), 0.0)
     members = mine_ref.shape[0]
@@ -127,19 +118,28 @@
         running = running + mine_ref[slot].astype(WIDE)
 
 
-def attend_kernel(query_ref, low_ref, intra_ref, cotangent_ref, gain_ref, attended_ref, sums_ref):
+def attend_kernel(
+    query_ref, key_ref, value_ref, low_ref, cotangent_ref, gain_ref, attended_ref, sums_ref, tiles_ref
+):
     rows, channels = query_ref.shape
-    squares = jnp.zeros((rows, DH), WIDE)
-    slopes = jnp.zeros((rows, DH), WIDE)
+    half = rows // 2
+    squares = [0.0, 0.0]
+    slopes = [0.0, 0.0]
     for head in range(channels // DH):
         at = head_columns(head)
-        attended = intra_ref[:, at] + dot(query_ref[:, at], state_of(low_ref, head), 1, 0)
-        attended_ref[:, at] = attended
-        squares = squares + attended * attended
-        slopes = slopes + cotangent_ref[:, at].astype(WIDE) * gain_ref[:, at] * attended
+        masked_tiles(query_ref, key_ref, at, tiles_ref, head)
+        intra = rows_product(tiles_ref, head, value_ref, at)
+        inter = dot(query_ref[:, at], state_of(low_ref, head), 1, 0)
+        for part in range(2):
+            at_rows = slice(part * half, (part + 1) * half)
+            attended = intra[part] + inter[at_rows]
+            attended_ref[at_rows, at] = attended
+            squares[part] = squares[part] + attended * attended
+            scaled = cotangent_ref[at_rows, at].astype(WIDE) * gain_ref[:, at]
+            slopes[part] = slopes[part] + scaled * attended
     parts = []
-    for sums in (squares, slopes):
-        for block in range(rows // DH):
+    for sums in squares + slopes:
+        for block in range(half // DH):
             turned = jnp.transpose(sums[block * DH : (block + 1) * DH])
             parts.append(jnp.sum(turned, axis=0, keepdims=True))
     packed = jnp.concatenate(parts, axis=0)
@@ -256,7 +256,7 @@
     line = lax.axis_size(LINE)
     mine = exchange(chunks, PLANE, PLANE_ORDER)
     (spread,) = call(totals_kernel, [((line,) + mine.shape[1:], LOW)], mine)
-    totals = exchange(spread, LINE, LINE_ORDER)
+    totals = exchange(spread, LINE, LINE_BACK_ORDER if backward else LINE_ORDER)
     extra = () if beside is None else tuple(beside(spread))
     order = extra[-1:]
     (low,) = call(
@@ -289,14 +289,10 @@
     )
     low, _ = scan_states(own, place, False)
     prefix_low = exchange(low, PLANE, PLANE_ORDER)
-    (intra,) = call(
-        intra_kernel, [whole], queries, key_vectors, values, low, flops=6 * unit,
-        places="vvva", scratch=[tiles],
-    )
     attended, sums = call(
         attend_kernel,
         [whole, ((members, 2 * rows // DH, DH), WIDE)],
-        queries, prefix_low, intra, cotangent, gain, flops=unit,
+        queries, key_vectors, values, prefix_low, cotangent, gain, flops=7 * unit, scratch=[tiles],
     )
     sums = exchange(sums, HEAD, HEAD_ORDER)
     grad, own_grad, inverse = call(

time: 97.1 us -> 94.3 us (0.971)
  starting transfers between devices: 16.3 us -> 6.9 us
  blocking collectives: 64.5 us -> 73.5 us
  waiting for transfers between devices: 1.42 us -> 0.01 us
    all_to_all x2 -> x1, starting transfers between devices: 16.3 us -> 6.9 us  [exchange(): return lax.all_to_all(blocks, axes, 0, 0, axis_index_groups=[order])]
    all_to_all x5 -> x6, blocking collectives: 64.5 us -> 73.5 us  [exchange(): return lax.all_to_all(blocks, axes, 0, 0, axis_index_groups=[order])]
    all_to_all x2 -> x1, waiting for transfers between devices: 1.42 us -> 0.01 us  [exchange(): return lax.all_to_all(blocks, axes, 0, 0, axis_index_groups=[order])]
    pallas_call x10 -> x9, Pallas kernels: 10.2 us -> 9.39 us  [call(): pl.pallas_call(kernel, out_shape=outs, in_specs=[kinds[k] for k in places...]
  transfers between devices with their start and end apart: 2 -> 1, of which waited for: 1 -> 0; matrix products, arithmetic and copies ran while one was open for 0% -> 0% of each run, Pallas kernels for 5% -> 4%
where the time goes in v5:
time: 94.3 us; the launch traced here: 93.7 us
  blocking collectives  73.5 us (78%)
  Pallas kernels  9.39 us (10%)
  starting transfers between devices  6.9 us (7%)
  local copies, waits for them, and re-layouts  3.19 us (3%)
    all_to_all x6, blocking collectives, exchange(): return lax.all_to_all(blocks, axes, 0, 0, axis_index_groups=[order])  73.5 us
    pallas_call x9, Pallas kernels, call(): pl.pallas_call(kernel, out_shape=outs, in_specs=[kinds[k] for k in places...  9.39 us
    all_to_all x1, starting transfers between devices, exchange(): return lax.all_to_all(blocks, axes, 0, 0, axis_index_groups=[order])  6.9 us
    unnamed x22, local copies, waits for them, and re-layouts  3.19 us
  transfers between devices with their start and end apart: 1, of which 0 were waited for; matrix products, arithmetic and copies ran while one was open for 0% of the time, Pallas kernels for 4%

profile of v5, /device:TPU:1, one launch (start us, length us, event | category | flops | bytes accessed | tf_op | source)
XLA Modules:
  0.0 93.7 jit_solution(3497131803242270458)
XLA Ops:
  0.6 0.0 copy-start.2
  0.6 0.0 copy-start.3
  0.7 1.8 %shard_map.84 = bf16[8,64,128]{2,1,0:T(8,128)(2,1)S(1)} custom-call(s32[1]{0:T(128)} %bitcast.place_ref, bf16[512,512]{1,0:T(8,128)(2,1)} %key_ref.5, bf16[512,512]{1,0:T(8,128)(2,1)} %value_ref.5), custom_call_target="tpu_custom_call" | custom-call | flops 67108864 | bytes 1179652 | tf_op jit(solution)/shard_map/pallas_call | solution.py:239
  2.5 13.7 %all_to_all.35.mine_ref = bf16[8,64,128]{2,1,0:T(8,128)(2,1)S(1)} all-to-all(bf16[8,64,128]{2,1,0:T(8,128)(2,1)S(1)} %shard_map.84), channel_id=1, replica_groups={{32,40,48,56,0,8,16,24},{33,41,49,57,1,9,17,25},{34,42,50,58,2,10,18,26..., dimensions={0} | all-to-all | bytes 262144 | tf_op jit(solution)/shard_map/all_to_all | solution.py:251
  16.1 0.0 copy-start.1
  16.2 0.0 copy-start
  16.2 15.8 %all_to_all.36.totals_ref = bf16[8,64,128]{2,1,0:T(8,128)(2,1)S(1)} all-to-all(bf16[8,64,128]{2,1,0:T(8,128)(2,1)S(1)} %shard_map.85), channel_id=1, replica_groups={{448,384,320,256,192,128,64,0},{449,385,321,257,193,129,65,1},{450,386,..., dimensions={0} | all-to-all | bytes 262144 | tf_op jit(solution)/shard_map/all_to_all | solution.py:251
  32.1 0.0 copy-start.8
  32.1 8.7 %all_to_all.37.low_ref = bf16[8,64,128]{2,1,0:T(8,128)(2,1)S(1)} all-to-all(bf16[8,64,128]{2,1,0:T(8,128)(2,1)S(1)} %shard_map.86), channel_id=1, replica_groups={{32,40,48,56,0,8,16,24},{33,41,49,57,1,9,17,25},{34,42,50,58,2,10,18,26..., dimensions={0} | all-to-all | bytes 262144 | tf_op jit(solution)/shard_map/all_to_all | solution.py:251
  40.7 0.0 copy-done.2
  40.8 0.0 copy-done.3
  40.8 0.0 copy-done.1
  40.8 0.0 copy-done
  40.8 0.0 copy-done.8
  40.8 1.4 %shard_map.87 = (f32[512,512]{1,0:T(8,128)S(1)}, f32[8,8,128]{2,1,0:T(8,128)S(1)}) custom-call(bf16[512,512]{1,0:T(8,128)(2,1)S(1)} %copy-done.3, bf16[512,512]{1,0:T(8,128)(2,1)S(1)} %copy-done, bf16[512,512]{1,0:T(8,128)(2,1)S(1)} %copy-done.1, bf16[8,64,128]{2,1,0:T(8,128)(2,1)S(1)} %all_to_all.37.low_ref, bf16[512,512]{1,0:T(8,128)(2,1)S(1)} %copy-done.2, ...), custom_call_target="tpu_custom_call" | custom-call | flops 469762048 | bytes 3311616 | tf_op jit(solution)/shard_map/pallas_call | solution.py:239
  42.2 0.0 copy-start.6
  42.2 16.1 %all_to_all.38.sums_ref = f32[8,8,128]{2,1,0:T(8,128)S(1)} all-to-all(f32[8,8,128]{2,1,0:T(8,128)S(1)} %get-tuple-element.15), channel_id=1, replica_groups={{5,7,1,3,4,6,0,2},{13,15,9,11,12,14,8,10},{21,23,17,19,20,22,16,18},{29..., dimensions={0} | all-to-all | bytes 65536 | tf_op jit(solution)/shard_map/all_to_all | solution.py:251
  58.4 0.6 shard_map.88
  59.0 0.0 copy-done.6
  59.0 0.0 copy-start.9
  59.0 9.7 %all_to_all.39.mine_ref = bf16[8,64,128]{2,1,0:T(8,128)(2,1)S(1)} all-to-all(bf16[8,64,128]{2,1,0:T(8,128)(2,1)S(1)} %get-tuple-element.19), channel_id=1, replica_groups={{32,40,48,56,0,8,16,24},{33,41,49,57,1,9,17,25},{34,42,50,58,2,10,18,26..., dimensions={0} | all-to-all | bytes 262144 | tf_op jit(solution)/shard_map/all_to_all | solution.py:251
  68.6 0.7 shard_map.89.after_ref
  69.3 0.0 copy-done.9
  69.3 6.9 %all-to-all-start.5 = ((bf16[8,64,128]{2,1,0:T(8,128)(2,1)}), bf16[8,64,128]{2,1,0:T(8,128)(2,1)S(1)}, u32[]{:S(2)}, u32[]{:S(2)}) async-start(bf16[8,64,128]{2,1,0:T(8,128)(2,1)} %shard_map.89.after_ref), calls=%async_computation.5 | async-start | bytes 262144 | tf_op jit(solution)/shard_map/all_to_all | solution.py:251
  76.2 0.0 copy-start.7
  76.2 1.2 %copy-done.7 = f32[512,512]{1,0:T(8,128)S(1)} copy-done((f32[512,512]{1,0:T(8,128)S(1)}, f32[512,512]{1,0:T(8,128)}, u32[]{:S(2)}) %copy-start.7) | copy-done | bytes 1048600
  77.4 0.0 copy-start.10
  77.4 0.9 %copy-done.10 = f32[512,128]{1,0:T(8,128)S(1)} copy-done((f32[512,128]{1,0:T(8,128)S(1)}, f32[512,128]{1,0:T(8,128)}, u32[]{:S(2)}) %copy-start.10) | copy-done | bytes 262168
  78.4 3.4 %shard_map.90 = (bf16[512,512]{1,0:T(8,128)(2,1)}, bf16[512,512]{1,0:T(8,128)(2,1)}, f32[512,512]{1,0:T(8,128)S(1)}, f32[512,512]{1,0:T(8,128)S(1)}) custom-call(bf16[512,512]{1,0:T(8,128)(2,1)S(1)} %get-tuple-element.17.grad_ref, bf16[512,512]{1,0:T(8,128)(2,1)S(1)} %copy-done.3, bf16[512,512]{1,0:T(8,128)(2,1)S(1)} %copy-done, ...), custom_call_target="tpu_custom_call" | custom-call | flops 1073741824 | bytes 6817792 | tf_op jit(solution)/shard_map/pallas_call | solution.py:239
  81.8 0.0 copy-start.4
  81.8 1.0 %copy-done.4 = f32[512,512]{1,0:T(8,128)} copy-done((f32[512,512]{1,0:T(8,128)}, f32[512,512]{1,0:T(8,128)S(1)}, u32[]{:S(2)}) %copy-start.4) | copy-done | bytes 1048600
  82.8 0.0 all-to-all-done.5.totals_ref
  82.8 0.0 copy-start.5
  82.8 9.5 %all_to_all.40.later_ref = bf16[8,64,128]{2,1,0:T(8,128)(2,1)S(1)} all-to-all(bf16[8,64,128]{2,1,0:T(8,128)(2,1)S(1)} %shard_map.91), channel_id=1, replica_groups={{32,40,48,56,0,8,16,24},{33,41,49,57,1,9,17,25},{34,42,50,58,2,10,18,26..., dimensions={0} | all-to-all | bytes 262144 | tf_op jit(solution)/shard_map/all_to_all | solution.py:251
  92.4 0.0 copy-done.5
  92.4 1.4 %shard_map.92 = (bf16[512,512]{1,0:T(8,128)(2,1)}, bf16[512,512]{1,0:T(8,128)(2,1)}) custom-call(bf16[512,512]{1,0:T(8,128)(2,1)S(1)} %copy-done, bf16[512,512]{1,0:T(8,128)(2,1)S(1)} %copy-done.1, bf16[8,64,128]{2,1,0:T(8,128)(2,1)S(1)} %all_to_all.40.later_ref, f32[512,512]{1,0:T(8,128)S(1)} %copy-done.5, ...), custom_call_target="tpu_custom_call" | custom-call | flops 134217728 | bytes 4325376 | tf_op jit(solution)/shard_map/pallas_call | solution.py:239
  (3 shorter events, 0.1 us)
Async XLA Ops:
  0.6 40.1 %copy-start.2 = (bf16[512,512]{1,0:T(8,128)(2,1)S(1)}, bf16[512,512]{1,0:T(8,128)(2,1)}, u32[]{:S(2)}) copy-start(bf16[512,512]{1,0:T(8,128)(2,1)} %cotangent_ref.3) | copy-start | bytes 1572868
  0.6 40.1 %copy-start.3 = (bf16[512,512]{1,0:T(8,128)(2,1)S(1)}, bf16[512,512]{1,0:T(8,128)(2,1)}, u32[]{:S(2)}) copy-start(bf16[512,512]{1,0:T(8,128)(2,1)} %query_ref.5) | copy-start | bytes 1572868
  16.1 24.6 %copy-start.1 = (bf16[512,512]{1,0:T(8,128)(2,1)S(1)}, bf16[512,512]{1,0:T(8,128)(2,1)}, u32[]{:S(2)}) copy-start(bf16[512,512]{1,0:T(8,128)(2,1)} %value_ref.5) | copy-start | bytes 1572868
  16.2 24.6 %copy-start = (bf16[512,512]{1,0:T(8,128)(2,1)S(1)}, bf16[512,512]{1,0:T(8,128)(2,1)}, u32[]{:S(2)}) copy-start(bf16[512,512]{1,0:T(8,128)(2,1)} %key_ref.5) | copy-start | bytes 1572868
  32.1 8.7 %copy-start.8 = (f32[512]{0:T(512)S(1)}, f32[512]{0:T(512)}, u32[]{:S(2)}) copy-start(f32[512]{0:T(512)} %param.8) | copy-start | bytes 6148
  42.2 16.7 %copy-start.6 = (f32[512,512]{1,0:T(8,128)}, f32[512,512]{1,0:T(8,128)S(1)}, u32[]{:S(2)}) copy-start(f32[512,512]{1,0:T(8,128)S(1)} %get-tuple-element.16.attended_ref) | copy-start | bytes 3145732
  59.0 10.3 %copy-start.9 = (f32[512,128]{1,0:T(8,128)}, f32[512,128]{1,0:T(8,128)S(1)}, u32[]{:S(2)}) copy-start(f32[512,128]{1,0:T(8,128)S(1)} %get-tuple-element.18.inverse_ref) | copy-start | bytes 786436
  69.3 13.5 %all-to-all-start.5 = ((bf16[8,64,128]{2,1,0:T(8,128)(2,1)}), bf16[8,64,128]{2,1,0:T(8,128)(2,1)S(1)}, u32[]{:S(2)}, u32[]{:S(2)}) async-start(bf16[8,64,128]{2,1,0:T(8,128)(2,1)} %shard_map.89.after_ref), calls=%async_computation.5 | async-start | bytes 262144 | tf_op jit(solution)/shard_map/all_to_all | solution.py:251
  76.2 1.2 %copy-start.7 = (f32[512,512]{1,0:T(8,128)S(1)}, f32[512,512]{1,0:T(8,128)}, u32[]{:S(2)}) copy-start(f32[512,512]{1,0:T(8,128)} %copy-done.6) | copy-start | bytes 3145732
  77.4 0.9 %copy-start.10 = (f32[512,128]{1,0:T(8,128)S(1)}, f32[512,128]{1,0:T(8,128)}, u32[]{:S(2)}) copy-start(f32[512,128]{1,0:T(8,128)} %copy-done.9) | copy-start | bytes 786436
  81.8 1.0 %copy-start.4 = (f32[512,512]{1,0:T(8,128)}, f32[512,512]{1,0:T(8,128)S(1)}, u32[]{:S(2)}) copy-start(f32[512,512]{1,0:T(8,128)S(1)} %get-tuple-element.23.key_part_ref) | copy-start | bytes 3145732
  82.8 9.6 %copy-start.5 = (f32[512,512]{1,0:T(8,128)S(1)}, f32[512,512]{1,0:T(8,128)}, u32[]{:S(2)}) copy-start(f32[512,512]{1,0:T(8,128)} %copy-done.4) | copy-start | bytes 3145732

commit v6 on v5

--- a/solution.py
+++ b/solution.py
@@ -13,8 +13,7 @@
 LINE = "z_lo"
 CTX = ("z_lo", "x", "core")
 HEAD = ("y", "z_hi")
-LINE_ORDER = [7, 6, 5, 4, 3, 2, 1, 0]
-LINE_BACK_ORDER = [4, 3, 5, 2, 6, 1, 7, 0]
+LINE_ORDER = [4, 3, 5, 2, 6, 1, 7, 0]
 PLANE_ORDER = [4, 5, 6, 7, 0, 1, 2, 3]
 HEAD_ORDER = [5, 7, 1, 3, 4, 6, 0, 2]
 LOW = jnp.bfloat16
@@ -59,18 +58,20 @@
         for side, (source, target) in enumerate(((left_hbm, left_ref), (right_hbm, right_ref))):
             copies.append(pltpu.make_async_copy(source.at[at], target.at[at], sems.at[side, block]))
             copies[-1].start()
-    half = rows // 2
-    for part in range(2):
-        for copy in copies[part * len(copies) // 2 : (part + 1) * len(copies) // 2]:
+    blocks = rows // DH
+    for block in range(blocks):
+        for copy in copies[2 * block : 2 * block + 2]:
             copy.wait()
-        at_rows = slice(part * half, (part + 1) * half)
+        at_rows = slice(block * DH, (block + 1) * DH)
         for head in range(channels // DH):
             at = head_columns(head)
             state = dot(left_ref[at_rows, at], right_ref[at_rows, at], 0, 0)
-            if part == 0:
+            if block > 0:
+                state = total_ref[head] + state
+            if block < blocks - 1:
                 total_ref[head] = state
             else:
-                put_state(out_ref, head, total_ref[head] + state)
+                put_state(out_ref, head, state)
 
 
 def masked_tiles(left_ref, right_ref, at, out_ref, head):
@@ -108,7 +109,7 @@
     out_ref = rest[-1]
     place = place_ref[0]
     running = jnp.zeros(mine_ref.shape[1:], WIDE)
-    for slot, plane in enumerate(LINE_BACK_ORDER if backward else LINE_ORDER):
+    for slot, plane in enumerate(LINE_ORDER):
         keep = plane > place if backward else plane < place
         running = running + jnp.where(keep, totals_ref[slot].astype(WIDE), 0.0)
     members = mine_ref.shape[0]
@@ -203,8 +204,9 @@
 ):
     rows, channels = key_ref.shape
     copies = []
-    for block in range(rows // DH):
-        at_rows = slice(block * DH, (block + 1) * DH)
+    step = rows // 2
+    for block in range(2):
+        at_rows = slice(block * step, (block + 1) * step)
         for head in range(channels // DH):
             at = head_columns(head)
             later = state_of(later_ref, head)
@@ -214,7 +216,7 @@
             value_grad_ref[at_rows, at] = (
                 value_part_ref[at_rows, at] + dot(key_ref[at_rows, at], later, 1, 0)
             ).astype(LOW)
-        span = pl.ds(block * DH, DH)
+        span = pl.ds(block * step, step)
         for side, (source, target) in enumerate(
             ((key_grad_ref, key_grad_hbm), (value_grad_ref, value_grad_hbm))
         ):
@@ -256,7 +258,7 @@
     line = lax.axis_size(LINE)
     mine = exchange(chunks, PLANE, PLANE_ORDER)
     (spread,) = call(totals_kernel, [((line,) + mine.shape[1:], LOW)], mine)
-    totals = exchange(spread, LINE, LINE_BACK_ORDER if backward else LINE_ORDER)
+    totals = exchange(spread, LINE, LINE_ORDER)
     extra = () if beside is None else tuple(beside(spread))
     order = extra[-1:]
     (low,) = call(

time: 94.3 us -> 93.6 us (level)
  no operation moved by 1% of the time
where the time goes in v6:
time: 93.6 us; the launch traced here: 93 us
  blocking collectives  73.2 us (78%)
  Pallas kernels  9.23 us (10%)
  starting transfers between devices  6.65 us (7%)
  local copies, waits for them, and re-layouts  3.19 us (3%)
    all_to_all x6, blocking collectives, exchange(): return lax.all_to_all(blocks, axes, 0, 0, axis_index_groups=[order])  73.2 us
    pallas_call x9, Pallas kernels, call(): pl.pallas_call(kernel, out_shape=outs, in_specs=[kinds[k] for k in places...  9.23 us
    all_to_all x1, starting transfers between devices, exchange(): return lax.all_to_all(blocks, axes, 0, 0, axis_index_groups=[order])  6.65 us
    unnamed x22, local copies, waits for them, and re-layouts  3.19 us
  transfers between devices with their start and end apart: 1, of which 0 were waited for; matrix products, arithmetic and copies ran while one was open for 0% of the time, Pallas kernels for 4%

profile of v6, /device:TPU:1, one launch (start us, length us, event | category | flops | bytes accessed | tf_op | source)
XLA Modules:
  0.0 93.0 jit_solution(7207330360150253798)
XLA Ops:
  0.6 0.0 copy-start.2
  0.6 0.0 copy-start.3
  0.7 1.7 %shard_map.84 = bf16[8,64,128]{2,1,0:T(8,128)(2,1)S(1)} custom-call(s32[1]{0:T(128)} %bitcast.place_ref, bf16[512,512]{1,0:T(8,128)(2,1)} %key_ref.5, bf16[512,512]{1,0:T(8,128)(2,1)} %value_ref.5), custom_call_target="tpu_custom_call" | custom-call | flops 67108864 | bytes 1179652 | tf_op jit(solution)/shard_map/pallas_call | solution.py:241
  2.3 13.7 %all_to_all.35.mine_ref = bf16[8,64,128]{2,1,0:T(8,128)(2,1)S(1)} all-to-all(bf16[8,64,128]{2,1,0:T(8,128)(2,1)S(1)} %shard_map.84), channel_id=1, replica_groups={{32,40,48,56,0,8,16,24},{33,41,49,57,1,9,17,25},{34,42,50,58,2,10,18,26..., dimensions={0} | all-to-all | bytes 262144 | tf_op jit(solution)/shard_map/all_to_all | solution.py:253
  16.0 0.0 copy-start.1
  16.1 0.0 copy-start
  16.1 13.1 %all_to_all.36.totals_ref = bf16[8,64,128]{2,1,0:T(8,128)(2,1)S(1)} all-to-all(bf16[8,64,128]{2,1,0:T(8,128)(2,1)S(1)} %shard_map.85), channel_id=1, replica_groups={{256,192,320,128,384,64,448,0},{257,193,321,129,385,65,449,1},{258,194,..., dimensions={0} | all-to-all | bytes 262144 | tf_op jit(solution)/shard_map/all_to_all | solution.py:253
  29.3 0.0 copy-start.8
  29.3 10.7 %all_to_all.37.low_ref = bf16[8,64,128]{2,1,0:T(8,128)(2,1)S(1)} all-to-all(bf16[8,64,128]{2,1,0:T(8,128)(2,1)S(1)} %shard_map.86), channel_id=1, replica_groups={{32,40,48,56,0,8,16,24},{33,41,49,57,1,9,17,25},{34,42,50,58,2,10,18,26..., dimensions={0} | all-to-all | bytes 262144 | tf_op jit(solution)/shard_map/all_to_all | solution.py:253
  40.0 0.0 copy-done.2
  40.0 0.0 copy-done.3
  40.0 0.0 copy-done.1
  40.0 0.0 copy-done
  40.0 0.0 copy-done.8
  40.0 1.4 %shard_map.87 = (f32[512,512]{1,0:T(8,128)S(1)}, f32[8,8,128]{2,1,0:T(8,128)S(1)}) custom-call(bf16[512,512]{1,0:T(8,128)(2,1)S(1)} %copy-done.3, bf16[512,512]{1,0:T(8,128)(2,1)S(1)} %copy-done, bf16[512,512]{1,0:T(8,128)(2,1)S(1)} %copy-done.1, bf16[8,64,128]{2,1,0:T(8,128)(2,1)S(1)} %all_to_all.37.low_ref, bf16[512,512]{1,0:T(8,128)(2,1)S(1)} %copy-done.2, ...), custom_call_target="tpu_custom_call" | custom-call | flops 469762048 | bytes 3311616 | tf_op jit(solution)/shard_map/pallas_call | solution.py:241
  41.5 0.0 copy-start.6
  41.5 16.5 %all_to_all.38.sums_ref = f32[8,8,128]{2,1,0:T(8,128)S(1)} all-to-all(f32[8,8,128]{2,1,0:T(8,128)S(1)} %get-tuple-element.15), channel_id=1, replica_groups={{5,7,1,3,4,6,0,2},{13,15,9,11,12,14,8,10},{21,23,17,19,20,22,16,18},{29..., dimensions={0} | all-to-all | bytes 65536 | tf_op jit(solution)/shard_map/all_to_all | solution.py:253
  58.0 0.6 shard_map.88
  58.5 0.0 copy-done.6
  58.6 0.0 copy-start.9
  58.6 9.7 %all_to_all.39.mine_ref = bf16[8,64,128]{2,1,0:T(8,128)(2,1)S(1)} all-to-all(bf16[8,64,128]{2,1,0:T(8,128)(2,1)S(1)} %get-tuple-element.19), channel_id=1, replica_groups={{32,40,48,56,0,8,16,24},{33,41,49,57,1,9,17,25},{34,42,50,58,2,10,18,26..., dimensions={0} | all-to-all | bytes 262144 | tf_op jit(solution)/shard_map/all_to_all | solution.py:253
  68.2 0.7 shard_map.89.after_ref
  68.9 0.0 copy-done.9
  68.9 6.6 %all-to-all-start.5 = ((bf16[8,64,128]{2,1,0:T(8,128)(2,1)}), bf16[8,64,128]{2,1,0:T(8,128)(2,1)S(1)}, u32[]{:S(2)}, u32[]{:S(2)}) async-start(bf16[8,64,128]{2,1,0:T(8,128)(2,1)} %shard_map.89.after_ref), calls=%async_computation.5 | async-start | bytes 262144 | tf_op jit(solution)/shard_map/all_to_all | solution.py:253
  75.6 0.0 copy-start.7
  75.6 1.2 %copy-done.7 = f32[512,512]{1,0:T(8,128)S(1)} copy-done((f32[512,512]{1,0:T(8,128)S(1)}, f32[512,512]{1,0:T(8,128)}, u32[]{:S(2)}) %copy-start.7) | copy-done | bytes 1048600
  76.8 0.0 copy-start.10
  76.8 0.9 %copy-done.10 = f32[512,128]{1,0:T(8,128)S(1)} copy-done((f32[512,128]{1,0:T(8,128)S(1)}, f32[512,128]{1,0:T(8,128)}, u32[]{:S(2)}) %copy-start.10) | copy-done | bytes 262168
  77.7 3.4 %shard_map.90 = (bf16[512,512]{1,0:T(8,128)(2,1)}, bf16[512,512]{1,0:T(8,128)(2,1)}, f32[512,512]{1,0:T(8,128)S(1)}, f32[512,512]{1,0:T(8,128)S(1)}) custom-call(bf16[512,512]{1,0:T(8,128)(2,1)S(1)} %get-tuple-element.17.grad_ref, bf16[512,512]{1,0:T(8,128)(2,1)S(1)} %copy-done.3, bf16[512,512]{1,0:T(8,128)(2,1)S(1)} %copy-done, ...), custom_call_target="tpu_custom_call" | custom-call | flops 1073741824 | bytes 6817792 | tf_op jit(solution)/shard_map/pallas_call | solution.py:241
  81.1 0.0 copy-start.4
  81.1 1.0 %copy-done.4 = f32[512,512]{1,0:T(8,128)} copy-done((f32[512,512]{1,0:T(8,128)}, f32[512,512]{1,0:T(8,128)S(1)}, u32[]{:S(2)}) %copy-start.4) | copy-done | bytes 1048600
  82.1 0.0 all-to-all-done.5.totals_ref
  82.1 0.0 copy-start.5
  82.2 9.5 %all_to_all.40.later_ref = bf16[8,64,128]{2,1,0:T(8,128)(2,1)S(1)} all-to-all(bf16[8,64,128]{2,1,0:T(8,128)(2,1)S(1)} %shard_map.91), channel_id=1, replica_groups={{32,40,48,56,0,8,16,24},{33,41,49,57,1,9,17,25},{34,42,50,58,2,10,18,26..., dimensions={0} | all-to-all | bytes 262144 | tf_op jit(solution)/shard_map/all_to_all | solution.py:253
  91.7 0.0 copy-done.5
  91.7 1.3 %shard_map.92 = (bf16[512,512]{1,0:T(8,128)(2,1)}, bf16[512,512]{1,0:T(8,128)(2,1)}) custom-call(bf16[512,512]{1,0:T(8,128)(2,1)S(1)} %copy-done, bf16[512,512]{1,0:T(8,128)(2,1)S(1)} %copy-done.1, bf16[8,64,128]{2,1,0:T(8,128)(2,1)S(1)} %all_to_all.40.later_ref, f32[512,512]{1,0:T(8,128)S(1)} %copy-done.5, ...), custom_call_target="tpu_custom_call" | custom-call | flops 134217728 | bytes 4325376 | tf_op jit(solution)/shard_map/pallas_call | solution.py:241
  (3 shorter events, 0.1 us)
Async XLA Ops:
  0.6 39.4 %copy-start.2 = (bf16[512,512]{1,0:T(8,128)(2,1)S(1)}, bf16[512,512]{1,0:T(8,128)(2,1)}, u32[]{:S(2)}) copy-start(bf16[512,512]{1,0:T(8,128)(2,1)} %cotangent_ref.3) | copy-start | bytes 1572868
  0.6 39.3 %copy-start.3 = (bf16[512,512]{1,0:T(8,128)(2,1)S(1)}, bf16[512,512]{1,0:T(8,128)(2,1)}, u32[]{:S(2)}) copy-start(bf16[512,512]{1,0:T(8,128)(2,1)} %query_ref.5) | copy-start | bytes 1572868
  16.0 24.0 %copy-start.1 = (bf16[512,512]{1,0:T(8,128)(2,1)S(1)}, bf16[512,512]{1,0:T(8,128)(2,1)}, u32[]{:S(2)}) copy-start(bf16[512,512]{1,0:T(8,128)(2,1)} %value_ref.5) | copy-start | bytes 1572868
  16.1 23.9 %copy-start = (bf16[512,512]{1,0:T(8,128)(2,1)S(1)}, bf16[512,512]{1,0:T(8,128)(2,1)}, u32[]{:S(2)}) copy-start(bf16[512,512]{1,0:T(8,128)(2,1)} %key_ref.5) | copy-start | bytes 1572868
  29.3 10.7 %copy-start.8 = (f32[512]{0:T(512)S(1)}, f32[512]{0:T(512)}, u32[]{:S(2)}) copy-start(f32[512]{0:T(512)} %param.8) | copy-start | bytes 6148
  41.5 17.1 %copy-start.6 = (f32[512,512]{1,0:T(8,128)}, f32[512,512]{1,0:T(8,128)S(1)}, u32[]{:S(2)}) copy-start(f32[512,512]{1,0:T(8,128)S(1)} %get-tuple-element.16.attended_ref) | copy-start | bytes 3145732
  58.6 10.3 %copy-start.9 = (f32[512,128]{1,0:T(8,128)}, f32[512,128]{1,0:T(8,128)S(1)}, u32[]{:S(2)}) copy-start(f32[512,128]{1,0:T(8,128)S(1)} %get-tuple-element.18.inverse_ref) | copy-start | bytes 786436
  68.9 13.2 %all-to-all-start.5 = ((bf16[8,64,128]{2,1,0:T(8,128)(2,1)}), bf16[8,64,128]{2,1,0:T(8,128)(2,1)S(1)}, u32[]{:S(2)}, u32[]{:S(2)}) async-start(bf16[8,64,128]{2,1,0:T(8,128)(2,1)} %shard_map.89.after_ref), calls=%async_computation.5 | async-start | bytes 262144 | tf_op jit(solution)/shard_map/all_to_all | solution.py:253
  75.6 1.2 %copy-start.7 = (f32[512,512]{1,0:T(8,128)S(1)}, f32[512,512]{1,0:T(8,128)}, u32[]{:S(2)}) copy-start(f32[512,512]{1,0:T(8,128)} %copy-done.6) | copy-start | bytes 3145732
  76.8 0.9 %copy-start.10 = (f32[512,128]{1,0:T(8,128)S(1)}, f32[512,128]{1,0:T(8,128)}, u32[]{:S(2)}) copy-start(f32[512,128]{1,0:T(8,128)} %copy-done.9) | copy-start | bytes 786436
  81.1 1.0 %copy-start.4 = (f32[512,512]{1,0:T(8,128)}, f32[512,512]{1,0:T(8,128)S(1)}, u32[]{:S(2)}) copy-start(f32[512,512]{1,0:T(8,128)S(1)} %get-tuple-element.23.key_part_ref) | copy-start | bytes 3145732
  82.1 9.6 %copy-start.5 = (f32[512,512]{1,0:T(8,128)S(1)}, f32[512,512]{1,0:T(8,128)}, u32[]{:S(2)}) copy-start(f32[512,512]{1,0:T(8,128)} %copy-done.4) | copy-start | bytes 3145732

commit v7 on v6

--- a/solution.py
+++ b/solution.py
@@ -13,8 +13,8 @@
 LINE = "z_lo"
 CTX = ("z_lo", "x", "core")
 HEAD = ("y", "z_hi")
-LINE_ORDER = [4, 3, 5, 2, 6, 1, 7, 0]
-PLANE_ORDER = [4, 5, 6, 7, 0, 1, 2, 3]
+LINE_ORDER = [4, 5, 6, 7, 0, 1, 2, 3]
+PLANE_ORDER = [5, 1, 0, 4, 7, 6, 3, 2]
 HEAD_ORDER = [5, 7, 1, 3, 4, 6, 0, 2]
 LOW = jnp.bfloat16
 WIDE = jnp.float32
@@ -120,16 +120,21 @@
 
 
 def attend_kernel(
-    query_ref, key_ref, value_ref, low_ref, cotangent_ref, gain_ref, attended_ref, sums_ref, tiles_ref
+    query_ref, key_ref, value_ref, low_ref, cotangent_ref, gain_ref, attended_ref, sums_ref
 ):
     rows, channels = query_ref.shape
     half = rows // 2
+    causal = causal_tile(half)
     squares = [0.0, 0.0]
     slopes = [0.0, 0.0]
     for head in range(channels // DH):
         at = head_columns(head)
-        masked_tiles(query_ref, key_ref, at, tiles_ref, head)
-        intra = rows_product(tiles_ref, head, value_ref, at)
+        first = dot(query_ref[:, at], key_ref[:half, at], 1, 1)
+        last = dot(query_ref[half:, at], key_ref[half:, at], 1, 1)
+        left = jnp.concatenate([jnp.where(causal, first[:half], 0.0), first[half:]]).astype(LOW)
+        left = dot(left, value_ref[:half, at], 1, 0)
+        last = jnp.where(causal, last, 0.0).astype(LOW)
+        intra = left[:half], left[half:] + dot(last, value_ref[half:, at], 1, 0)
         inter = dot(query_ref[:, at], state_of(low_ref, head), 1, 0)
         for part in range(2):
             at_rows = slice(part * half, (part + 1) * half)
@@ -294,7 +299,7 @@
     attended, sums = call(
         attend_kernel,
         [whole, ((members, 2 * rows // DH, DH), WIDE)],
-        queries, key_vectors, values, prefix_low, cotangent, gain, flops=7 * unit, scratch=[tiles],
+        queries, key_vectors, values, prefix_low, cotangent, gain, flops=7 * unit,
     )
     sums = exchange(sums, HEAD, HEAD_ORDER)
     grad, own_grad, inverse = call(

time: 93.6 us -> 90.6 us (0.968)
  blocking collectives: 73.2 us -> 70.3 us
    all_to_all x6, blocking collectives: 73.2 us -> 70.3 us  [exchange(): return lax.all_to_all(blocks, axes, 0, 0, axis_index_groups=[order])]
where the time goes in v7:
time: 90.6 us; the launch traced here: 90.1 us
  blocking collectives  70.3 us (78%)
  Pallas kernels  9.23 us (10%)
  starting transfers between devices  6.65 us (7%)
  local copies, waits for them, and re-layouts  3.19 us (4%)
    all_to_all x6, blocking collectives, exchange(): return lax.all_to_all(blocks, axes, 0, 0, axis_index_groups=[order])  70.3 us
    pallas_call x9, Pallas kernels, call(): pl.pallas_call(kernel, out_shape=outs, in_specs=[kinds[k] for k in places...  9.23 us
    all_to_all x1, starting transfers between devices, exchange(): return lax.all_to_all(blocks, axes, 0, 0, axis_index_groups=[order])  6.65 us
    unnamed x22, local copies, waits for them, and re-layouts  3.19 us
  transfers between devices with their start and end apart: 1, of which 0 were waited for; matrix products, arithmetic and copies ran while one was open for 0% of the time, Pallas kernels for 4%

profile of v7, /device:TPU:1, one launch (start us, length us, event | category | flops | bytes accessed | tf_op | source)
XLA Modules:
  0.0 90.1 jit_solution(12865767574420392502)
XLA Ops:
  0.6 0.0 copy-start.2
  0.6 0.0 copy-start.3
  0.7 1.7 %shard_map.84 = bf16[8,64,128]{2,1,0:T(8,128)(2,1)S(1)} custom-call(s32[1]{0:T(128)} %bitcast.place_ref, bf16[512,512]{1,0:T(8,128)(2,1)} %key_ref.5, bf16[512,512]{1,0:T(8,128)(2,1)} %value_ref.5), custom_call_target="tpu_custom_call" | custom-call | flops 67108864 | bytes 1179652 | tf_op jit(solution)/shard_map/pallas_call | solution.py:246
  2.3 13.6 %all_to_all.35.mine_ref = bf16[8,64,128]{2,1,0:T(8,128)(2,1)S(1)} all-to-all(bf16[8,64,128]{2,1,0:T(8,128)(2,1)S(1)} %shard_map.84), channel_id=1, replica_groups={{40,8,0,32,56,48,24,16},{41,9,1,33,57,49,25,17},{42,10,2,34,58,50,26,18..., dimensions={0} | all-to-all | bytes 262144 | tf_op jit(solution)/shard_map/all_to_all | solution.py:258
  15.9 0.0 copy-start.1
  16.0 0.0 copy-start
  16.0 13.0 %all_to_all.36.totals_ref = bf16[8,64,128]{2,1,0:T(8,128)(2,1)S(1)} all-to-all(bf16[8,64,128]{2,1,0:T(8,128)(2,1)S(1)} %shard_map.85), channel_id=1, replica_groups={{256,320,384,448,0,64,128,192},{257,321,385,449,1,65,129,193},{258,322,..., dimensions={0} | all-to-all | bytes 262144 | tf_op jit(solution)/shard_map/all_to_all | solution.py:258
  29.1 0.0 copy-start.8
  29.1 9.8 %all_to_all.37.low_ref = bf16[8,64,128]{2,1,0:T(8,128)(2,1)S(1)} all-to-all(bf16[8,64,128]{2,1,0:T(8,128)(2,1)S(1)} %shard_map.86), channel_id=1, replica_groups={{40,8,0,32,56,48,24,16},{41,9,1,33,57,49,25,17},{42,10,2,34,58,50,26,18..., dimensions={0} | all-to-all | bytes 262144 | tf_op jit(solution)/shard_map/all_to_all | solution.py:258
  38.8 0.0 copy-done.2
  38.8 0.0 copy-done.3
  38.9 0.0 copy-done.1
  38.9 0.0 copy-done
  38.9 0.0 copy-done.8
  38.9 1.4 %shard_map.87 = (f32[512,512]{1,0:T(8,128)S(1)}, f32[8,8,128]{2,1,0:T(8,128)S(1)}) custom-call(bf16[512,512]{1,0:T(8,128)(2,1)S(1)} %copy-done.3, bf16[512,512]{1,0:T(8,128)(2,1)S(1)} %copy-done, bf16[512,512]{1,0:T(8,128)(2,1)S(1)} %copy-done.1, bf16[8,64,128]{2,1,0:T(8,128)(2,1)S(1)} %all_to_all.37.low_ref, bf16[512,512]{1,0:T(8,128)(2,1)S(1)} %copy-done.2, ...), custom_call_target="tpu_custom_call" | custom-call | flops 469762048 | bytes 3311616 | tf_op jit(solution)/shard_map/pallas_call | solution.py:246
  40.3 0.0 copy-start.6
  40.3 16.5 %all_to_all.38.sums_ref = f32[8,8,128]{2,1,0:T(8,128)S(1)} all-to-all(f32[8,8,128]{2,1,0:T(8,128)S(1)} %get-tuple-element.15), channel_id=1, replica_groups={{5,7,1,3,4,6,0,2},{13,15,9,11,12,14,8,10},{21,23,17,19,20,22,16,18},{29..., dimensions={0} | all-to-all | bytes 65536 | tf_op jit(solution)/shard_map/all_to_all | solution.py:258
  56.8 0.6 shard_map.88
  57.4 0.0 copy-done.6
  57.4 0.0 copy-start.9
  57.4 8.8 %all_to_all.39.mine_ref = bf16[8,64,128]{2,1,0:T(8,128)(2,1)S(1)} all-to-all(bf16[8,64,128]{2,1,0:T(8,128)(2,1)S(1)} %get-tuple-element.19), channel_id=1, replica_groups={{40,8,0,32,56,48,24,16},{41,9,1,33,57,49,25,17},{42,10,2,34,58,50,26,18..., dimensions={0} | all-to-all | bytes 262144 | tf_op jit(solution)/shard_map/all_to_all | solution.py:258
  66.3 0.7 shard_map.89.after_ref
  66.9 0.0 copy-done.9
  67.0 6.6 %all-to-all-start.5 = ((bf16[8,64,128]{2,1,0:T(8,128)(2,1)}), bf16[8,64,128]{2,1,0:T(8,128)(2,1)S(1)}, u32[]{:S(2)}, u32[]{:S(2)}) async-start(bf16[8,64,128]{2,1,0:T(8,128)(2,1)} %shard_map.89.after_ref), calls=%async_computation.5 | async-start | bytes 262144 | tf_op jit(solution)/shard_map/all_to_all | solution.py:258
  73.6 0.0 copy-start.7
  73.6 1.2 %copy-done.7 = f32[512,512]{1,0:T(8,128)S(1)} copy-done((f32[512,512]{1,0:T(8,128)S(1)}, f32[512,512]{1,0:T(8,128)}, u32[]{:S(2)}) %copy-start.7) | copy-done | bytes 1048600
  74.8 0.0 copy-start.10
  74.8 0.9 %copy-done.10 = f32[512,128]{1,0:T(8,128)S(1)} copy-done((f32[512,128]{1,0:T(8,128)S(1)}, f32[512,128]{1,0:T(8,128)}, u32[]{:S(2)}) %copy-start.10) | copy-done | bytes 262168
  75.8 3.4 %shard_map.90 = (bf16[512,512]{1,0:T(8,128)(2,1)}, bf16[512,512]{1,0:T(8,128)(2,1)}, f32[512,512]{1,0:T(8,128)S(1)}, f32[512,512]{1,0:T(8,128)S(1)}) custom-call(bf16[512,512]{1,0:T(8,128)(2,1)S(1)} %get-tuple-element.17.grad_ref, bf16[512,512]{1,0:T(8,128)(2,1)S(1)} %copy-done.3, bf16[512,512]{1,0:T(8,128)(2,1)S(1)} %copy-done, ...), custom_call_target="tpu_custom_call" | custom-call | flops 1073741824 | bytes 6817792 | tf_op jit(solution)/shard_map/pallas_call | solution.py:246
  79.2 0.0 copy-start.4
  79.2 1.0 %copy-done.4 = f32[512,512]{1,0:T(8,128)} copy-done((f32[512,512]{1,0:T(8,128)}, f32[512,512]{1,0:T(8,128)S(1)}, u32[]{:S(2)}) %copy-start.4) | copy-done | bytes 1048600
  80.2 0.0 all-to-all-done.5.totals_ref
  80.2 0.0 copy-start.5
  80.2 8.5 %all_to_all.40.later_ref = bf16[8,64,128]{2,1,0:T(8,128)(2,1)S(1)} all-to-all(bf16[8,64,128]{2,1,0:T(8,128)(2,1)S(1)} %shard_map.91), channel_id=1, replica_groups={{40,8,0,32,56,48,24,16},{41,9,1,33,57,49,25,17},{42,10,2,34,58,50,26,18..., dimensions={0} | all-to-all | bytes 262144 | tf_op jit(solution)/shard_map/all_to_all | solution.py:258
  88.7 0.0 copy-done.5
  88.7 1.3 %shard_map.92 = (bf16[512,512]{1,0:T(8,128)(2,1)}, bf16[512,512]{1,0:T(8,128)(2,1)}) custom-call(bf16[512,512]{1,0:T(8,128)(2,1)S(1)} %copy-done, bf16[512,512]{1,0:T(8,128)(2,1)S(1)} %copy-done.1, bf16[8,64,128]{2,1,0:T(8,128)(2,1)S(1)} %all_to_all.40.later_ref, f32[512,512]{1,0:T(8,128)S(1)} %copy-done.5, ...), custom_call_target="tpu_custom_call" | custom-call | flops 134217728 | bytes 4325376 | tf_op jit(solution)/shard_map/pallas_call | solution.py:246
  (3 shorter events, 0.1 us)
Async XLA Ops:
  0.6 38.2 %copy-start.2 = (bf16[512,512]{1,0:T(8,128)(2,1)S(1)}, bf16[512,512]{1,0:T(8,128)(2,1)}, u32[]{:S(2)}) copy-start(bf16[512,512]{1,0:T(8,128)(2,1)} %cotangent_ref.3) | copy-start | bytes 1572868
  0.6 38.2 %copy-start.3 = (bf16[512,512]{1,0:T(8,128)(2,1)S(1)}, bf16[512,512]{1,0:T(8,128)(2,1)}, u32[]{:S(2)}) copy-start(bf16[512,512]{1,0:T(8,128)(2,1)} %query_ref.5) | copy-start | bytes 1572868
  15.9 22.9 %copy-start.1 = (bf16[512,512]{1,0:T(8,128)(2,1)S(1)}, bf16[512,512]{1,0:T(8,128)(2,1)}, u32[]{:S(2)}) copy-start(bf16[512,512]{1,0:T(8,128)(2,1)} %value_ref.5) | copy-start | bytes 1572868
  16.0 22.9 %copy-start = (bf16[512,512]{1,0:T(8,128)(2,1)S(1)}, bf16[512,512]{1,0:T(8,128)(2,1)}, u32[]{:S(2)}) copy-start(bf16[512,512]{1,0:T(8,128)(2,1)} %key_ref.5) | copy-start | bytes 1572868
  29.1 9.8 %copy-start.8 = (f32[512]{0:T(512)S(1)}, f32[512]{0:T(512)}, u32[]{:S(2)}) copy-start(f32[512]{0:T(512)} %param.8) | copy-start | bytes 6148
  40.3 17.1 %copy-start.6 = (f32[512,512]{1,0:T(8,128)}, f32[512,512]{1,0:T(8,128)S(1)}, u32[]{:S(2)}) copy-start(f32[512,512]{1,0:T(8,128)S(1)} %get-tuple-element.16.attended_ref) | copy-start | bytes 3145732
  57.4 9.5 %copy-start.9 = (f32[512,128]{1,0:T(8,128)}, f32[512,128]{1,0:T(8,128)S(1)}, u32[]{:S(2)}) copy-start(f32[512,128]{1,0:T(8,128)S(1)} %get-tuple-element.18.inverse_ref) | copy-start | bytes 786436
  67.0 13.2 %all-to-all-start.5 = ((bf16[8,64,128]{2,1,0:T(8,128)(2,1)}), bf16[8,64,128]{2,1,0:T(8,128)(2,1)S(1)}, u32[]{:S(2)}, u32[]{:S(2)}) async-start(bf16[8,64,128]{2,1,0:T(8,128)(2,1)} %shard_map.89.after_ref), calls=%async_computation.5 | async-start | bytes 262144 | tf_op jit(solution)/shard_map/all_to_all | solution.py:258
  73.6 1.2 %copy-start.7 = (f32[512,512]{1,0:T(8,128)S(1)}, f32[512,512]{1,0:T(8,128)}, u32[]{:S(2)}) copy-start(f32[512,512]{1,0:T(8,128)} %copy-done.6) | copy-start | bytes 3145732
  74.8 0.9 %copy-start.10 = (f32[512,128]{1,0:T(8,128)S(1)}, f32[512,128]{1,0:T(8,128)}, u32[]{:S(2)}) copy-start(f32[512,128]{1,0:T(8,128)} %copy-done.9) | copy-start | bytes 786436
  79.2 1.0 %copy-start.4 = (f32[512,512]{1,0:T(8,128)}, f32[512,512]{1,0:T(8,128)S(1)}, u32[]{:S(2)}) copy-start(f32[512,512]{1,0:T(8,128)S(1)} %get-tuple-element.23.key_part_ref) | copy-start | bytes 3145732
  80.2 8.6 %copy-start.5 = (f32[512,512]{1,0:T(8,128)S(1)}, f32[512,512]{1,0:T(8,128)}, u32[]{:S(2)}) copy-start(f32[512,512]{1,0:T(8,128)} %copy-done.4) | copy-start | bytes 3145732

commit v8 on v7

--- a/solution.py
+++ b/solution.py
@@ -164,11 +164,11 @@
     mean = total * (1.0 / full_width)
     inverse = lax.rsqrt(mean[:blocks] + EPSILON)
     factor = inverse * inverse * inverse * mean[blocks:]
+    inverse_ref[...] = inverse
     for block in range(blocks):
         at_rows = slice(block * DH, (block + 1) * DH)
         wide = jnp.transpose(jnp.broadcast_to(inverse[block : block + 1], (DH, DH)))
         second = jnp.transpose(jnp.broadcast_to(factor[block : block + 1], (DH, DH)))
-        inverse_ref[at_rows] = wide
         for head in range(channels // DH):
             at = head_columns(head)
             scaled = cotangent_ref[at_rows, at].astype(WIDE) * gain_ref[:, at]
@@ -185,7 +185,10 @@
     query_grad_ref, normed_ref, key_part_ref, value_part_ref, tiles_ref, grad_tiles_ref,
 ):
     half = grad_ref.shape[0] // 2
-    inverse = inverse_ref[...]
+    turned = []
+    for block in range(inverse_ref.shape[0]):
+        turned.append(jnp.transpose(jnp.broadcast_to(inverse_ref[block : block + 1], (DH, DH))))
+    inverse = jnp.concatenate(turned, axis=0)
     for head in range(grad_ref.shape[1] // DH):
         at = head_columns(head)
         masked_tiles(query_ref, key_ref, at, tiles_ref, head)
@@ -304,7 +307,7 @@
     sums = exchange(sums, HEAD, HEAD_ORDER)
     grad, own_grad, inverse = call(
         functools.partial(grad_kernel, full_width),
-        [result, chunks, ((rows, DH), WIDE)],
+        [result, chunks, ((rows // DH, DH), WIDE)],
         sums, attended, cotangent, gain, queries, flops=unit,
     )
 

time: 90.6 us -> 90.6 us (level)
  blocking collectives: 70.3 us -> 71.4 us
  local copies, waits for them, and re-layouts: 3.19 us -> 2.24 us
    all_to_all x6, blocking collectives: 70.3 us -> 71.4 us  [exchange(): return lax.all_to_all(blocks, axes, 0, 0, axis_index_groups=[order])]
    unnamed x22 -> x18, local copies, waits for them, and re-layouts: 3.19 us -> 2.24 us
where the time goes in v8:
time: 90.6 us; the launch traced here: 90.1 us
  blocking collectives  71.4 us (79%)
  Pallas kernels  9.06 us (10%)
  starting transfers between devices  6.65 us (7%)
  local copies, waits for them, and re-layouts  2.24 us (2%)
    all_to_all x6, blocking collectives, exchange(): return lax.all_to_all(blocks, axes, 0, 0, axis_index_groups=[order])  71.4 us
    pallas_call x9, Pallas kernels, call(): pl.pallas_call(kernel, out_shape=outs, in_specs=[kinds[k] for k in places...  9.06 us
    all_to_all x1, starting transfers between devices, exchange(): return lax.all_to_all(blocks, axes, 0, 0, axis_index_groups=[order])  6.65 us
    unnamed x18, local copies, waits for them, and re-layouts  2.24 us
  transfers between devices with their start and end apart: 1, of which 0 were waited for; matrix products, arithmetic and copies ran while one was open for 0% of the time, Pallas kernels for 4%

profile of v8, /device:TPU:1, one launch (start us, length us, event | category | flops | bytes accessed | tf_op | source)
XLA Modules:
  0.0 90.1 jit_solution(10938740776855364976)
XLA Ops:
  0.6 0.0 copy-start.2
  0.6 0.0 copy-start.3
  0.7 1.7 %shard_map.84 = bf16[8,64,128]{2,1,0:T(8,128)(2,1)S(1)} custom-call(s32[1]{0:T(128)} %bitcast.place_ref, bf16[512,512]{1,0:T(8,128)(2,1)} %key_ref.5, bf16[512,512]{1,0:T(8,128)(2,1)} %value_ref.5), custom_call_target="tpu_custom_call" | custom-call | flops 67108864 | bytes 1179652 | tf_op jit(solution)/shard_map/pallas_call | solution.py:249
  2.3 13.6 %all_to_all.35.mine_ref = bf16[8,64,128]{2,1,0:T(8,128)(2,1)S(1)} all-to-all(bf16[8,64,128]{2,1,0:T(8,128)(2,1)S(1)} %shard_map.84), channel_id=1, replica_groups={{40,8,0,32,56,48,24,16},{41,9,1,33,57,49,25,17},{42,10,2,34,58,50,26,18..., dimensions={0} | all-to-all | bytes 262144 | tf_op jit(solution)/shard_map/all_to_all | solution.py:261
  15.9 0.0 copy-start.1
  16.0 0.0 copy-start
  16.0 13.0 %all_to_all.36.totals_ref = bf16[8,64,128]{2,1,0:T(8,128)(2,1)S(1)} all-to-all(bf16[8,64,128]{2,1,0:T(8,128)(2,1)S(1)} %shard_map.85), channel_id=1, replica_groups={{256,320,384,448,0,64,128,192},{257,321,385,449,1,65,129,193},{258,322,..., dimensions={0} | all-to-all | bytes 262144 | tf_op jit(solution)/shard_map/all_to_all | solution.py:261
  29.1 0.0 copy-start.8
  29.1 9.8 %all_to_all.37.low_ref = bf16[8,64,128]{2,1,0:T(8,128)(2,1)S(1)} all-to-all(bf16[8,64,128]{2,1,0:T(8,128)(2,1)S(1)} %shard_map.86), channel_id=1, replica_groups={{40,8,0,32,56,48,24,16},{41,9,1,33,57,49,25,17},{42,10,2,34,58,50,26,18..., dimensions={0} | all-to-all | bytes 262144 | tf_op jit(solution)/shard_map/all_to_all | solution.py:261
  38.8 0.0 copy-done.2
  38.8 0.0 copy-done.3
  38.9 0.0 copy-done.1
  38.9 0.0 copy-done
  38.9 0.0 copy-done.8
  38.9 1.4 %shard_map.87 = (f32[512,512]{1,0:T(8,128)S(1)}, f32[8,8,128]{2,1,0:T(8,128)S(1)}) custom-call(bf16[512,512]{1,0:T(8,128)(2,1)S(1)} %copy-done.3, bf16[512,512]{1,0:T(8,128)(2,1)S(1)} %copy-done, bf16[512,512]{1,0:T(8,128)(2,1)S(1)} %copy-done.1, bf16[8,64,128]{2,1,0:T(8,128)(2,1)S(1)} %all_to_all.37.low_ref, bf16[512,512]{1,0:T(8,128)(2,1)S(1)} %copy-done.2, ...), custom_call_target="tpu_custom_call" | custom-call | flops 469762048 | bytes 3311616 | tf_op jit(solution)/shard_map/pallas_call | solution.py:249
  40.3 0.0 copy-start.6
  40.3 16.5 %all_to_all.38.sums_ref = f32[8,8,128]{2,1,0:T(8,128)S(1)} all-to-all(f32[8,8,128]{2,1,0:T(8,128)S(1)} %get-tuple-element.15), channel_id=1, replica_groups={{5,7,1,3,4,6,0,2},{13,15,9,11,12,14,8,10},{21,23,17,19,20,22,16,18},{29..., dimensions={0} | all-to-all | bytes 65536 | tf_op jit(solution)/shard_map/all_to_all | solution.py:261
  56.8 0.6 shard_map.88
  57.4 0.0 copy-done.6
  57.4 8.8 %all_to_all.39.mine_ref = bf16[8,64,128]{2,1,0:T(8,128)(2,1)S(1)} all-to-all(bf16[8,64,128]{2,1,0:T(8,128)(2,1)S(1)} %get-tuple-element.19), channel_id=1, replica_groups={{40,8,0,32,56,48,24,16},{41,9,1,33,57,49,25,17},{42,10,2,34,58,50,26,18..., dimensions={0} | all-to-all | bytes 262144 | tf_op jit(solution)/shard_map/all_to_all | solution.py:261
  66.3 0.7 shard_map.89.after_ref
  66.9 6.6 %all-to-all-start.5 = ((bf16[8,64,128]{2,1,0:T(8,128)(2,1)}), bf16[8,64,128]{2,1,0:T(8,128)(2,1)S(1)}, u32[]{:S(2)}, u32[]{:S(2)}) async-start(bf16[8,64,128]{2,1,0:T(8,128)(2,1)} %shard_map.89.after_ref), calls=%async_computation.5 | async-start | bytes 262144 | tf_op jit(solution)/shard_map/all_to_all | solution.py:261
  73.6 0.0 copy-start.7
  73.6 1.2 %copy-done.7 = f32[512,512]{1,0:T(8,128)S(1)} copy-done((f32[512,512]{1,0:T(8,128)S(1)}, f32[512,512]{1,0:T(8,128)}, u32[]{:S(2)}) %copy-start.7) | copy-done | bytes 1048600
  74.8 3.2 %shard_map.90 = (bf16[512,512]{1,0:T(8,128)(2,1)}, bf16[512,512]{1,0:T(8,128)(2,1)}, f32[512,512]{1,0:T(8,128)S(1)}, f32[512,512]{1,0:T(8,128)S(1)}) custom-call(bf16[512,512]{1,0:T(8,128)(2,1)S(1)} %get-tuple-element.17.grad_ref, bf16[512,512]{1,0:T(8,128)(2,1)S(1)} %copy-done.3, bf16[512,512]{1,0:T(8,128)(2,1)S(1)} %copy-done, ...), custom_call_target="tpu_custom_call" | custom-call | flops 1073741824 | bytes 6557696 | tf_op jit(solution)/shard_map/pallas_call | solution.py:249
  78.0 0.0 copy-start.4
  78.0 1.0 %copy-done.4 = f32[512,512]{1,0:T(8,128)} copy-done((f32[512,512]{1,0:T(8,128)}, f32[512,512]{1,0:T(8,128)S(1)}, u32[]{:S(2)}) %copy-start.4) | copy-done | bytes 1048600
  79.0 0.0 all-to-all-done.5.totals_ref
  79.0 0.0 copy-start.5
  79.1 9.6 %all_to_all.40.later_ref = bf16[8,64,128]{2,1,0:T(8,128)(2,1)S(1)} all-to-all(bf16[8,64,128]{2,1,0:T(8,128)(2,1)S(1)} %shard_map.91), channel_id=1, replica_groups={{40,8,0,32,56,48,24,16},{41,9,1,33,57,49,25,17},{42,10,2,34,58,50,26,18..., dimensions={0} | all-to-all | bytes 262144 | tf_op jit(solution)/shard_map/all_to_all | solution.py:261
  88.7 0.0 copy-done.5
  88.7 1.3 %shard_map.92 = (bf16[512,512]{1,0:T(8,128)(2,1)}, bf16[512,512]{1,0:T(8,128)(2,1)}) custom-call(bf16[512,512]{1,0:T(8,128)(2,1)S(1)} %copy-done, bf16[512,512]{1,0:T(8,128)(2,1)S(1)} %copy-done.1, bf16[8,64,128]{2,1,0:T(8,128)(2,1)S(1)} %all_to_all.40.later_ref, f32[512,512]{1,0:T(8,128)S(1)} %copy-done.5, ...), custom_call_target="tpu_custom_call" | custom-call | flops 134217728 | bytes 4325376 | tf_op jit(solution)/shard_map/pallas_call | solution.py:249
  (3 shorter events, 0.1 us)
Async XLA Ops:
  0.6 38.2 %copy-start.2 = (bf16[512,512]{1,0:T(8,128)(2,1)S(1)}, bf16[512,512]{1,0:T(8,128)(2,1)}, u32[]{:S(2)}) copy-start(bf16[512,512]{1,0:T(8,128)(2,1)} %cotangent_ref.3) | copy-start | bytes 1572868
  0.6 38.2 %copy-start.3 = (bf16[512,512]{1,0:T(8,128)(2,1)S(1)}, bf16[512,512]{1,0:T(8,128)(2,1)}, u32[]{:S(2)}) copy-start(bf16[512,512]{1,0:T(8,128)(2,1)} %query_ref.5) | copy-start | bytes 1572868
  15.9 22.9 %copy-start.1 = (bf16[512,512]{1,0:T(8,128)(2,1)S(1)}, bf16[512,512]{1,0:T(8,128)(2,1)}, u32[]{:S(2)}) copy-start(bf16[512,512]{1,0:T(8,128)(2,1)} %value_ref.5) | copy-start | bytes 1572868
  16.0 22.9 %copy-start = (bf16[512,512]{1,0:T(8,128)(2,1)S(1)}, bf16[512,512]{1,0:T(8,128)(2,1)}, u32[]{:S(2)}) copy-start(bf16[512,512]{1,0:T(8,128)(2,1)} %key_ref.5) | copy-start | bytes 1572868
  29.1 9.8 %copy-start.8 = (f32[512]{0:T(512)S(1)}, f32[512]{0:T(512)}, u32[]{:S(2)}) copy-start(f32[512]{0:T(512)} %param.8) | copy-start | bytes 6148
  40.3 17.1 %copy-start.6 = (f32[512,512]{1,0:T(8,128)}, f32[512,512]{1,0:T(8,128)S(1)}, u32[]{:S(2)}) copy-start(f32[512,512]{1,0:T(8,128)S(1)} %get-tuple-element.16.attended_ref) | copy-start | bytes 3145732
  66.9 12.1 %all-to-all-start.5 = ((bf16[8,64,128]{2,1,0:T(8,128)(2,1)}), bf16[8,64,128]{2,1,0:T(8,128)(2,1)S(1)}, u32[]{:S(2)}, u32[]{:S(2)}) async-start(bf16[8,64,128]{2,1,0:T(8,128)(2,1)} %shard_map.89.after_ref), calls=%async_computation.5 | async-start | bytes 262144 | tf_op jit(solution)/shard_map/all_to_all | solution.py:261
  73.6 1.2 %copy-start.7 = (f32[512,512]{1,0:T(8,128)S(1)}, f32[512,512]{1,0:T(8,128)}, u32[]{:S(2)}) copy-start(f32[512,512]{1,0:T(8,128)} %copy-done.6) | copy-start | bytes 3145732
  78.0 1.0 %copy-start.4 = (f32[512,512]{1,0:T(8,128)}, f32[512,512]{1,0:T(8,128)S(1)}, u32[]{:S(2)}) copy-start(f32[512,512]{1,0:T(8,128)S(1)} %get-tuple-element.23.key_part_ref) | copy-start | bytes 3145732
  79.0 9.7 %copy-start.5 = (f32[512,512]{1,0:T(8,128)S(1)}, f32[512,512]{1,0:T(8,128)}, u32[]{:S(2)}) copy-start(f32[512,512]{1,0:T(8,128)} %copy-done.4) | copy-start | bytes 3145732

commit v9 on v7

--- a/solution.py
+++ b/solution.py
@@ -14,7 +14,7 @@
 CTX = ("z_lo", "x", "core")
 HEAD = ("y", "z_hi")
 LINE_ORDER = [4, 5, 6, 7, 0, 1, 2, 3]
-PLANE_ORDER = [5, 1, 0, 4, 7, 6, 3, 2]
+PLANE_ORDER = [5, 7, 1, 3, 2, 0, 6, 4]
 HEAD_ORDER = [5, 7, 1, 3, 4, 6, 0, 2]
 LOW = jnp.bfloat16
 WIDE = jnp.float32

time: 90.6 us -> 90.5 us (level)
  no operation moved by 1% of the time
where the time goes in v9:
time: 90.5 us; the launch traced here: 90 us
  blocking collectives  70.2 us (78%)
  Pallas kernels  9.23 us (10%)
  starting transfers between devices  6.65 us (7%)
  local copies, waits for them, and re-layouts  3.19 us (4%)
    all_to_all x6, blocking collectives, exchange(): return lax.all_to_all(blocks, axes, 0, 0, axis_index_groups=[order])  70.2 us
    pallas_call x9, Pallas kernels, call(): pl.pallas_call(kernel, out_shape=outs, in_specs=[kinds[k] for k in places...  9.23 us
    all_to_all x1, starting transfers between devices, exchange(): return lax.all_to_all(blocks, axes, 0, 0, axis_index_groups=[order])  6.65 us
    unnamed x22, local copies, waits for them, and re-layouts  3.19 us
  transfers between devices with their start and end apart: 1, of which 0 were waited for; matrix products, arithmetic and copies ran while one was open for 0% of the time, Pallas kernels for 4%

profile of v9, /device:TPU:1, one launch (start us, length us, event | category | flops | bytes accessed | tf_op | source)
XLA Modules:
  0.0 90.0 jit_solution(7714087128765324306)
XLA Ops:
  0.6 0.0 copy-start.2
  0.6 0.0 copy-start.3
  0.7 1.7 %shard_map.84 = bf16[8,64,128]{2,1,0:T(8,128)(2,1)S(1)} custom-call(s32[1]{0:T(128)} %bitcast.place_ref, bf16[512,512]{1,0:T(8,128)(2,1)} %key_ref.5, bf16[512,512]{1,0:T(8,128)(2,1)} %value_ref.5), custom_call_target="tpu_custom_call" | custom-call | flops 67108864 | bytes 1179652 | tf_op jit(solution)/shard_map/pallas_call | solution.py:246
  2.3 13.7 %all_to_all.35.mine_ref = bf16[8,64,128]{2,1,0:T(8,128)(2,1)S(1)} all-to-all(bf16[8,64,128]{2,1,0:T(8,128)(2,1)S(1)} %shard_map.84), channel_id=1, replica_groups={{40,56,8,24,16,0,48,32},{41,57,9,25,17,1,49,33},{42,58,10,26,18,2,50,34..., dimensions={0} | all-to-all | bytes 262144 | tf_op jit(solution)/shard_map/all_to_all | solution.py:258
  16.0 0.0 copy-start.1
  16.0 0.0 copy-start
  16.0 13.0 %all_to_all.36.totals_ref = bf16[8,64,128]{2,1,0:T(8,128)(2,1)S(1)} all-to-all(bf16[8,64,128]{2,1,0:T(8,128)(2,1)S(1)} %shard_map.85), channel_id=1, replica_groups={{256,320,384,448,0,64,128,192},{257,321,385,449,1,65,129,193},{258,322,..., dimensions={0} | all-to-all | bytes 262144 | tf_op jit(solution)/shard_map/all_to_all | solution.py:258
  29.1 0.0 copy-start.8
  29.2 9.7 %all_to_all.37.low_ref = bf16[8,64,128]{2,1,0:T(8,128)(2,1)S(1)} all-to-all(bf16[8,64,128]{2,1,0:T(8,128)(2,1)S(1)} %shard_map.86), channel_id=1, replica_groups={{40,56,8,24,16,0,48,32},{41,57,9,25,17,1,49,33},{42,58,10,26,18,2,50,34..., dimensions={0} | all-to-all | bytes 262144 | tf_op jit(solution)/shard_map/all_to_all | solution.py:258
  38.8 0.0 copy-done.2
  38.8 0.0 copy-done.3
  38.8 0.0 copy-done.1
  38.8 0.0 copy-done
  38.9 0.0 copy-done.8
  38.9 1.4 %shard_map.87 = (f32[512,512]{1,0:T(8,128)S(1)}, f32[8,8,128]{2,1,0:T(8,128)S(1)}) custom-call(bf16[512,512]{1,0:T(8,128)(2,1)S(1)} %copy-done.3, bf16[512,512]{1,0:T(8,128)(2,1)S(1)} %copy-done, bf16[512,512]{1,0:T(8,128)(2,1)S(1)} %copy-done.1, bf16[8,64,128]{2,1,0:T(8,128)(2,1)S(1)} %all_to_all.37.low_ref, bf16[512,512]{1,0:T(8,128)(2,1)S(1)} %copy-done.2, ...), custom_call_target="tpu_custom_call" | custom-call | flops 469762048 | bytes 3311616 | tf_op jit(solution)/shard_map/pallas_call | solution.py:246
  40.3 0.0 copy-start.6
  40.3 16.5 %all_to_all.38.sums_ref = f32[8,8,128]{2,1,0:T(8,128)S(1)} all-to-all(f32[8,8,128]{2,1,0:T(8,128)S(1)} %get-tuple-element.15), channel_id=1, replica_groups={{5,7,1,3,4,6,0,2},{13,15,9,11,12,14,8,10},{21,23,17,19,20,22,16,18},{29..., dimensions={0} | all-to-all | bytes 65536 | tf_op jit(solution)/shard_map/all_to_all | solution.py:258
  56.8 0.6 shard_map.88
  57.4 0.0 copy-done.6
  57.4 0.0 copy-start.9
  57.4 8.6 %all_to_all.39.mine_ref = bf16[8,64,128]{2,1,0:T(8,128)(2,1)S(1)} all-to-all(bf16[8,64,128]{2,1,0:T(8,128)(2,1)S(1)} %get-tuple-element.19), channel_id=1, replica_groups={{40,56,8,24,16,0,48,32},{41,57,9,25,17,1,49,33},{42,58,10,26,18,2,50,34..., dimensions={0} | all-to-all | bytes 262144 | tf_op jit(solution)/shard_map/all_to_all | solution.py:258
  66.0 0.7 shard_map.89.after_ref
  66.7 0.0 copy-done.9
  66.7 6.6 %all-to-all-start.5 = ((bf16[8,64,128]{2,1,0:T(8,128)(2,1)}), bf16[8,64,128]{2,1,0:T(8,128)(2,1)S(1)}, u32[]{:S(2)}, u32[]{:S(2)}) async-start(bf16[8,64,128]{2,1,0:T(8,128)(2,1)} %shard_map.89.after_ref), calls=%async_computation.5 | async-start | bytes 262144 | tf_op jit(solution)/shard_map/all_to_all | solution.py:258
  73.3 0.0 copy-start.7
  73.3 1.2 %copy-done.7 = f32[512,512]{1,0:T(8,128)S(1)} copy-done((f32[512,512]{1,0:T(8,128)S(1)}, f32[512,512]{1,0:T(8,128)}, u32[]{:S(2)}) %copy-start.7) | copy-done | bytes 1048600
  74.5 0.0 copy-start.10
  74.5 0.9 %copy-done.10 = f32[512,128]{1,0:T(8,128)S(1)} copy-done((f32[512,128]{1,0:T(8,128)S(1)}, f32[512,128]{1,0:T(8,128)}, u32[]{:S(2)}) %copy-start.10) | copy-done | bytes 262168
  75.5 3.4 %shard_map.90 = (bf16[512,512]{1,0:T(8,128)(2,1)}, bf16[512,512]{1,0:T(8,128)(2,1)}, f32[512,512]{1,0:T(8,128)S(1)}, f32[512,512]{1,0:T(8,128)S(1)}) custom-call(bf16[512,512]{1,0:T(8,128)(2,1)S(1)} %get-tuple-element.17.grad_ref, bf16[512,512]{1,0:T(8,128)(2,1)S(1)} %copy-done.3, bf16[512,512]{1,0:T(8,128)(2,1)S(1)} %copy-done, ...), custom_call_target="tpu_custom_call" | custom-call | flops 1073741824 | bytes 6817792 | tf_op jit(solution)/shard_map/pallas_call | solution.py:246
  78.9 0.0 copy-start.4
  78.9 1.0 %copy-done.4 = f32[512,512]{1,0:T(8,128)} copy-done((f32[512,512]{1,0:T(8,128)}, f32[512,512]{1,0:T(8,128)S(1)}, u32[]{:S(2)}) %copy-start.4) | copy-done | bytes 1048600
  79.9 0.0 all-to-all-done.5.totals_ref
  79.9 0.0 copy-start.5
  79.9 8.7 %all_to_all.40.later_ref = bf16[8,64,128]{2,1,0:T(8,128)(2,1)S(1)} all-to-all(bf16[8,64,128]{2,1,0:T(8,128)(2,1)S(1)} %shard_map.91), channel_id=1, replica_groups={{40,56,8,24,16,0,48,32},{41,57,9,25,17,1,49,33},{42,58,10,26,18,2,50,34..., dimensions={0} | all-to-all | bytes 262144 | tf_op jit(solution)/shard_map/all_to_all | solution.py:258
  88.6 0.0 copy-done.5
  88.6 1.3 %shard_map.92 = (bf16[512,512]{1,0:T(8,128)(2,1)}, bf16[512,512]{1,0:T(8,128)(2,1)}) custom-call(bf16[512,512]{1,0:T(8,128)(2,1)S(1)} %copy-done, bf16[512,512]{1,0:T(8,128)(2,1)S(1)} %copy-done.1, bf16[8,64,128]{2,1,0:T(8,128)(2,1)S(1)} %all_to_all.40.later_ref, f32[512,512]{1,0:T(8,128)S(1)} %copy-done.5, ...), custom_call_target="tpu_custom_call" | custom-call | flops 134217728 | bytes 4325376 | tf_op jit(solution)/shard_map/pallas_call | solution.py:246
  (3 shorter events, 0.1 us)
Async XLA Ops:
  0.6 38.2 %copy-start.2 = (bf16[512,512]{1,0:T(8,128)(2,1)S(1)}, bf16[512,512]{1,0:T(8,128)(2,1)}, u32[]{:S(2)}) copy-start(bf16[512,512]{1,0:T(8,128)(2,1)} %cotangent_ref.3) | copy-start | bytes 1572868
  0.6 38.2 %copy-start.3 = (bf16[512,512]{1,0:T(8,128)(2,1)S(1)}, bf16[512,512]{1,0:T(8,128)(2,1)}, u32[]{:S(2)}) copy-start(bf16[512,512]{1,0:T(8,128)(2,1)} %query_ref.5) | copy-start | bytes 1572868
  16.0 22.8 %copy-start.1 = (bf16[512,512]{1,0:T(8,128)(2,1)S(1)}, bf16[512,512]{1,0:T(8,128)(2,1)}, u32[]{:S(2)}) copy-start(bf16[512,512]{1,0:T(8,128)(2,1)} %value_ref.5) | copy-start | bytes 1572868
  16.0 22.8 %copy-start = (bf16[512,512]{1,0:T(8,128)(2,1)S(1)}, bf16[512,512]{1,0:T(8,128)(2,1)}, u32[]{:S(2)}) copy-start(bf16[512,512]{1,0:T(8,128)(2,1)} %key_ref.5) | copy-start | bytes 1572868
  29.1 9.7 %copy-start.8 = (f32[512]{0:T(512)S(1)}, f32[512]{0:T(512)}, u32[]{:S(2)}) copy-start(f32[512]{0:T(512)} %param.8) | copy-start | bytes 6148
  40.3 17.1 %copy-start.6 = (f32[512,512]{1,0:T(8,128)}, f32[512,512]{1,0:T(8,128)S(1)}, u32[]{:S(2)}) copy-start(f32[512,512]{1,0:T(8,128)S(1)} %get-tuple-element.16.attended_ref) | copy-start | bytes 3145732
  57.4 9.3 %copy-start.9 = (f32[512,128]{1,0:T(8,128)}, f32[512,128]{1,0:T(8,128)S(1)}, u32[]{:S(2)}) copy-start(f32[512,128]{1,0:T(8,128)S(1)} %get-tuple-element.18.inverse_ref) | copy-start | bytes 786436
  66.7 13.2 %all-to-all-start.5 = ((bf16[8,64,128]{2,1,0:T(8,128)(2,1)}), bf16[8,64,128]{2,1,0:T(8,128)(2,1)S(1)}, u32[]{:S(2)}, u32[]{:S(2)}) async-start(bf16[8,64,128]{2,1,0:T(8,128)(2,1)} %shard_map.89.after_ref), calls=%async_computation.5 | async-start | bytes 262144 | tf_op jit(solution)/shard_map/all_to_all | solution.py:258
  73.3 1.2 %copy-start.7 = (f32[512,512]{1,0:T(8,128)S(1)}, f32[512,512]{1,0:T(8,128)}, u32[]{:S(2)}) copy-start(f32[512,512]{1,0:T(8,128)} %copy-done.6) | copy-start | bytes 3145732
  74.5 0.9 %copy-start.10 = (f32[512,128]{1,0:T(8,128)S(1)}, f32[512,128]{1,0:T(8,128)}, u32[]{:S(2)}) copy-start(f32[512,128]{1,0:T(8,128)} %copy-done.9) | copy-start | bytes 786436
  78.9 1.0 %copy-start.4 = (f32[512,512]{1,0:T(8,128)}, f32[512,512]{1,0:T(8,128)S(1)}, u32[]{:S(2)}) copy-start(f32[512,512]{1,0:T(8,128)S(1)} %get-tuple-element.23.key_part_ref) | copy-start | bytes 3145732
  79.9 8.8 %copy-start.5 = (f32[512,512]{1,0:T(8,128)S(1)}, f32[512,512]{1,0:T(8,128)}, u32[]{:S(2)}) copy-start(f32[512,512]{1,0:T(8,128)} %copy-done.4) | copy-start | bytes 3145732
